TPU v7x, 256 devices: a whole 4x4x8 slice. The times are simulated.
256 devices in a mesh: kv: 32 (over z, x), head: 8 (over y, core).
Axes of the slice: x: 4, y: 4, z: 8, core: 2. Of those that a mesh axis runs over, the one named last changes fastest.
Arguments:
- tokens: bfloat16 [2, 8, 8192], P(None, None, 'kv'), may hold values from -3 to 3
- norm_attn: bfloat16 [8192], P('kv'), may hold values from 0.099609375 to 1.8984375
- norm_ffn: bfloat16 [8192], P('kv'), may hold values from 0.099609375 to 1.8984375
- w_query: bfloat16 [8192, 8192], P('kv', 'head'), may hold values from -0.0625 to 0.0625
- w_kv: bfloat16 [8192, 2, 1024], P('kv', None, 'head'), may hold values from -0.0625 to 0.0625
- w_out: bfloat16 [8192, 8192], P('head', 'kv'), may hold values from -0.0625 to 0.0625
- w_gate_up: bfloat16 [8192, 2, 28672], P('kv', None, 'head'), may hold values from -0.0625 to 0.0625
- w_down: bfloat16 [28672, 8192], P('head', 'kv'), may hold values from -0.03125 to 0.03125
- cache_keys: bfloat16 [8, 8, 32768, 128], P(None, 'head', 'kv'), may hold values from -400 to 400
- cache_values: bfloat16 [8, 8, 32768, 128], P(None, 'head', 'kv'), may hold values from -6 to 6
- lengths: int32 [8], replicated, may hold values from 4096 to 32768, as said below
- owner: int32 [2], replicated, may hold values from 0 to 31
Outputs:
- layer_out: bfloat16 [2, 8, 8192], P(None, None, 'kv')
- stored: bfloat16 [32, 2, 8, 8, 2, 128], P('kv', None, None, 'head')
Inputs may be any that keep to these rules, and one draw needn't show every extreme that they name: `lengths`: at least one rollout has all 32768 positions cached.
All inputs are finite; a program needn't handle non-finite values.
Results may differ from a plain program's by a relative error of at most 0.014.
The roundings to bfloat16 on the way count: a program that leaves them out, or rounds other values in their place, can miss the bound.
Values may be sent and summed in bfloat16 or wider, within the bound.
No kernel may reach another device: no remote copies, remote signals or barrier semaphores. Data moves between devices by JAX's collectives and lax.ppermute only.
A program may use at most 64 MiB of HBM per device.

v0:
```python
import jax
import jax.numpy as jnp
from jax import lax
from jax.sharding import PartitionSpec as P

D = 8192


EPSILON = 1e-05
NEGATIVE = -1e30


def absorb(carry, scores, keep, values, form):
    running, totals, sums = carry
    scores = jnp.where(keep, scores, NEGATIVE)
    updated = jnp.maximum(running, jnp.max(scores, -1))
    weights = jnp.where(keep, jnp.exp(scores - updated[..., None]), 0.0)
    factor = jnp.exp(running - updated)
    totals = totals * factor + jnp.sum(weights, -1)
    sums = sums * factor[..., None] + jnp.einsum(
        form, weights.astype(jnp.bfloat16), values, preferred_element_type=jnp.float32
    )
    return (updated, totals, sums)


def attend(query, new_kv, row_steps, cache_keys, cache_values, lengths, owner, kv_index):
    span = cache_keys.shape[2]
    head_size = cache_keys.shape[3]
    block = min(512, span)
    scale = head_size ** (-0.5)
    live = jnp.clip(lengths - kv_index * span, 0, span)
    block_count = (jnp.max(live) + block - 1) // block
    lead = query.shape[:4]
    start = (
        jnp.full(lead, NEGATIVE, jnp.float32),
        jnp.zeros(lead, jnp.float32),
        jnp.zeros(query.shape, jnp.float32),
    )

    def visit_block(block_index, carry):
        keys = lax.dynamic_slice_in_dim(cache_keys, block_index * block, block, 2)
        values = lax.dynamic_slice_in_dim(cache_values, block_index * block, block, 2)
        scores = (
            jnp.einsum("sbngd,bncd->sbngc", query, keys, preferred_element_type=jnp.float32) * scale
        )
        places = block_index * block + jnp.arange(block, dtype=jnp.int32)
        keep = (places[None, :] < live[:, None])[None, :, None, None, :]
        return absorb(carry, scores, keep, values, "sbngc,bncd->sbngd")

    carry = lax.fori_loop(0, block_count, visit_block, start)
    new_steps = jnp.arange(new_kv.shape[0], dtype=jnp.int32)
    wanted = jnp.array(row_steps, jnp.int32)
    scores = (
        jnp.einsum("sbngd,tbnd->sbngt", query, new_kv[:, :, 0], preferred_element_type=jnp.float32)
        * scale
    )
    holder = jnp.take(owner, new_steps) == kv_index
    keep = ((new_steps[None, :] <= wanted[:, None]) & holder[None, :])[:, None, None, None, :]
    return absorb(carry, scores, keep, new_kv[:, :, 1], "sbngt,tbnd->sbngd")


def shards(
    tokens,
    norm_attn,
    norm_ffn,
    w_query,
    w_kv,
    w_out,
    w_gate_up,
    w_down,
    cache_keys,
    cache_values,
    lengths,
    owner,
):
    kv_index = lax.axis_index("kv")
    step_total = tokens.shape[0]
    pieces = []
    new_kv = None
    for step_index in range(step_total):
        row_block = tokens[step_index : step_index + 1]
        earlier = new_kv
        step_count, rollouts, width_local = row_block.shape
        row_count = step_count * rollouts
        heads_local = cache_keys.shape[1]
        head_size = cache_keys.shape[3]
        flat = row_block.astype(jnp.float32).reshape(row_count, width_local)
        normed = (flat * norm_attn.astype(jnp.float32)).astype(jnp.bfloat16)
        query_part = jnp.dot(normed, w_query, preferred_element_type=jnp.float32)
        kv_part = jnp.dot(normed, w_kv.reshape(width_local, -1), preferred_element_type=jnp.float32)
        square_part = jnp.sum(flat * flat, -1)
        query_sum, kv_sum, square_sum = lax.psum((query_part, kv_part, square_part), "kv")
        inv_attn = lax.rsqrt(square_sum / D + EPSILON)[:, None]
        query = (
            (query_sum * inv_attn)
            .astype(jnp.bfloat16)
            .reshape(step_count, rollouts, heads_local, -1, head_size)
        )
        fresh = (
            (kv_sum * inv_attn)
            .astype(jnp.bfloat16)
            .reshape(step_count, rollouts, 2, heads_local, head_size)
        )
        run_new_kv = fresh if earlier is None else jnp.concatenate([earlier, fresh], 0)
        running, totals, sums = attend(
            query, run_new_kv, [step_index], cache_keys, cache_values, lengths, owner, kv_index
        )
        largest = lax.pmax(running, "kv")
        factor = jnp.exp(running - largest)
        totals, sums = lax.psum((totals * factor, sums * factor[..., None]), "kv")
        context = (sums / totals[..., None]).astype(jnp.bfloat16).reshape(row_count, -1)
        attn_part = jnp.dot(context, w_out, preferred_element_type=jnp.float32)
        resid = flat + lax.psum(attn_part, "head")
        normed_two = (resid * norm_ffn.astype(jnp.float32)).astype(jnp.bfloat16)
        gate_up_part = jnp.dot(
            normed_two, w_gate_up.reshape(width_local, -1), preferred_element_type=jnp.float32
        ).reshape(row_count, 2, -1)
        square_two = jnp.sum(resid * resid, -1)
        gate_sum, square_total = lax.psum((gate_up_part, square_two), "kv")
        inv_ffn = lax.rsqrt(square_total / D + EPSILON)[:, None]
        hidden = (jax.nn.silu(gate_sum[:, 0] * inv_ffn) * (gate_sum[:, 1] * inv_ffn)).astype(
            jnp.bfloat16
        )
        down_part = jnp.dot(hidden, w_down, preferred_element_type=jnp.float32)
        down_sum = lax.psum(down_part, "head")
        result = (resid + down_sum).astype(jnp.bfloat16).reshape(step_count, rollouts, width_local)
        new_kv = run_new_kv
        pieces.append(result)
    layer_out = jnp.concatenate(pieces, 0)
    mine = owner == kv_index
    placed = jnp.where(
        mine[:, None, None, None, None],
        new_kv.transpose(0, 1, 3, 2, 4),
        jnp.zeros((), jnp.bfloat16),
    )
    return (layer_out, placed[None])


def solution(mesh):
    return jax.shard_map(
        shards,
        mesh=mesh,
        in_specs=(
            P(None, None, "kv"),
            P("kv"),
            P("kv"),
            P("kv", "head"),
            P("kv", None, "head"),
            P("head", "kv"),
            P("kv", None, "head"),
            P("head", "kv"),
            P(None, "head", "kv", None),
            P(None, "head", "kv", None),
            P(),
            P(),
        ),
        out_specs=(P(None, None, "kv"), P("kv", None, None, "head", None, None)),
        check_vma=False,
    )
```

profile of v0, /device:TPU:1, one launch (start us, length us, event | category | flops | bytes accessed | tf_op | source)
XLA Modules:
  0.0 946.6 jit_solution(12952805226543108505)
XLA Ops:
  7.2 1.5 fusion.154
  10.1 1.2 fusion.105
  11.3 1.2 fusion.109
  12.6 0.8 fusion.83
  13.4 1.1 fusion.44
  14.4 118.7 %all-reduce.4 = (f32[8,1024]{1,0:T(8,128)S(1)}, f32[8]{0:T(128)S(1)}, f32[8,256]{1,0:T(8,128)S(1)}) all-reduce(f32[8,1024]{1,0:T(8,128)S(1)} %fusion.109, f32[8]{0:T(128)S(1)} %fusion.83, f32[8,256]{1,0:T(8,128)S(1)} %fusion.44), channel_id=1, replica_groups=mesh['kv'=32,'head'=8] {'kv'}, use_global_device_ids=true, to_apply=%region_1.0 | all-reduce | flops 10248 | bytes 81984 | tf_op jit(solution)/shard_map/psum | solution.py:92
  133.3 7.1 while.30
  133.4 1.7 fusion.179
  135.3 1.5 fusion.182
  137.0 1.7 fusion.179
  138.9 1.5 fusion.182
  140.7 55.7 %pmax.14 = f32[1,8,1,8]{3,1,2,0:T(8,128)S(1)} all-reduce(f32[1,8,1,8]{3,1,2,0:T(8,128)S(1)} %get-tuple-element.229), channel_id=1, replica_groups=mesh['kv'=32,'head'=8] {'kv'}, use_global_device_ids=true, to_apply=%region_9.10 | all-reduce | flops 64 | bytes 512 | tf_op jit(solution)/shard_map/pmax | solution.py:108
  196.6 4.4 copy.47
  201.0 6.0 copy.32
  207.1 111.9 %all-reduce.3 = (f32[1,8,1,8,128]{4,3,1,0,2:T(8,128)S(1)}, f32[8,8]{1,0:T(8,128)S(1)}) all-reduce(f32[1,8,1,8,128]{4,3,1,0,2:T(8,128)S(1)} %fusion.64, f32[8,8]{1,0:T(8,128)S(1)} %get-tuple-element.246), channel_id=1, replica_groups=mesh['kv'=32,'head'=8] {'kv'}, use_global_device_ids=true, to_apply=%region_10.11 | all-reduce | flops 8256 | bytes 66048 | tf_op jit(solution)/shard_map/psum | solution.py:110
  319.2 82.4 %psum.131 = f32[8,256]{1,0:T(8,128)S(1)} all-reduce(f32[8,256]{1,0:T(8,128)S(1)} %fusion.68), channel_id=1, replica_groups=mesh['kv'=32,'head'=8] {'head'}, use_global_device_ids=true, to_apply=%region_12.13 | all-reduce | flops 2048 | bytes 16384 | tf_op jit(solution)/shard_map/psum | solution.py:113
  401.8 110.7 %all-reduce.2 = (f32[8,1024]{1,0:T(8,128)S(1)}, f32[8]{0:T(128)S(1)}, f32[8,256]{1,0:T(8,128)S(1)}) all-reduce(f32[8,1024]{1,0:T(8,128)S(1)} %fusion.105, f32[8]{0:T(128)S(1)} %get-tuple-element.169, f32[8,256]{1,0:T(8,128)S(1)} %fusion.42), channel_id=1, replica_groups=mesh['kv'=32,'head'=8] {'kv'}, use_global_device_ids=true, to_apply=%region_17.18 | all-reduce | flops 10248 | bytes 81984 | tf_op jit(solution)/shard_map/psum | solution.py:92
  512.6 7.1 while.31
  512.7 1.7 fusion.185
  514.6 1.5 fusion.188
  516.3 1.7 fusion.185
  518.2 1.5 fusion.188
  520.7 55.9 %pmax.15 = f32[1,8,1,8]{3,1,2,0:T(8,128)S(1)} all-reduce(f32[1,8,1,8]{3,1,2,0:T(8,128)S(1)} %get-tuple-element.227), channel_id=1, replica_groups=mesh['kv'=32,'head'=8] {'kv'}, use_global_device_ids=true, to_apply=%region_26.27 | all-reduce | flops 64 | bytes 512 | tf_op jit(solution)/shard_map/pmax | solution.py:108
  576.9 111.6 %all-reduce.1 = (f32[1,8,1,8,128]{4,3,1,0,2:T(8,128)S(1)}, f32[8,8]{1,0:T(8,128)S(1)}) all-reduce(f32[1,8,1,8,128]{4,3,1,0,2:T(8,128)S(1)} %fusion.41, f32[8,8]{1,0:T(8,128)S(1)} %get-tuple-element.244), channel_id=1, replica_groups=mesh['kv'=32,'head'=8] {'kv'}, use_global_device_ids=true, to_apply=%region_27.28 | all-reduce | flops 8256 | bytes 66048 | tf_op jit(solution)/shard_map/psum | solution.py:110
  688.7 81.3 %psum.140 = f32[8,256]{1,0:T(8,128)S(1)} all-reduce(f32[8,256]{1,0:T(8,128)S(1)} %fusion.65), channel_id=1, replica_groups=mesh['kv'=32,'head'=8] {'head'}, use_global_device_ids=true, to_apply=%region_30.31 | all-reduce | flops 2048 | bytes 16384 | tf_op jit(solution)/shard_map/psum | solution.py:113
  770.1 3.9 fusion.95
  774.0 1.8 fusion.100
  776.0 55.7 %all-reduce = (f32[8]{0:T(128)S(1)}, f32[8]{0:T(128)S(1)}) all-reduce(f32[8]{0:T(128)S(1)} %multiply_reduce_fusion, f32[8]{0:T(128)S(1)} %get-tuple-element.168), channel_id=1, replica_groups=mesh['kv'=32,'head'=8] {'kv'}, use_global_device_ids=true, to_apply=%region_33.34 | all-reduce | flops 16 | bytes 128 | tf_op jit(solution)/shard_map/psum | solution.py:119
  832.3 78.7 %all-reduce.9.cloned.1.call-done = (f32[8,2,3584]{2,0,1:T(8,128)}, f32[8,2,3584]{2,0,1:T(8,128)}) async-done(((f32[8,2,3584]{2,0,1:T(8,128)}, f32[8,2,3584]{2,0,1:T(8,128)}), (f32[8,2,3584]{2,0,1:T(8,128)}, f32[8,2,3584]{2,0,1:T(8,128)})) %all-reduce.9.cloned.1.call-update) | async-done | bytes 458768 | tf_op jit(solution)/shard_map/psum | solution.py:119
  911.0 1.3 fusion.58
  912.3 1.4 fusion.56
  913.7 25.4 %all-reduce.6 = (f32[8,256]{1,0:T(8,128)S(1)}, f32[8,256]{1,0:T(8,128)S(1)}) all-reduce(f32[8,256]{1,0:T(8,128)S(1)} %fusion.58, f32[8,256]{1,0:T(8,128)S(1)} %fusion.56), channel_id=1, replica_groups=mesh['kv'=32,'head'=8] {'head'}, use_global_device_ids=true, to_apply=%region_34.35 | all-reduce | flops 4096 | bytes 32768 | tf_op jit(solution)/shard_map/psum | solution.py:125
  (87 shorter events, 5.9 us)
Async XLA Ops:
  7.2 903.8 %copy-start = (bf16[3584,256]{1,0:T(8,128)(2,1)S(1)}, bf16[3584,256]{1,0:T(8,128)(2,1)}, u32[]{:S(2)}) copy-start(bf16[3584,256]{1,0:T(8,128)(2,1)} %param.25) | copy-start | bytes 5505028
  7.2 903.8 %all-reduce.9.cloned.1.call-start = ((), (), s32[]{:S(2)}) async-start(), calls=%async_computation | async-start | bytes 917504 | tf_op jit(solution)/shard_map/psum | solution.py:119
  133.3 7.4 copy-start.1
  133.3 63.2 %copy-start.4 = (bf16[256,2,128]{2,1,0:T(2,128)(2,1)S(1)}, bf16[256,2,128]{2,1,0:T(2,128)(2,1)}, u32[]{:S(2)}) copy-start(bf16[256,2,128]{2,1,0:T(2,128)(2,1)} %param.22) | copy-start | bytes 393220
  133.3 63.1 %copy-start.5 = (bf16[2,8,256]{2,1,0:T(8,128)(2,1)S(1)}, bf16[2,8,256]{2,1,0:T(8,128)(2,1)}, u32[]{:S(2)}) copy-start(bf16[2,8,256]{2,1,0:T(8,128)(2,1)} %param.18) | copy-start | bytes 24580
  201.0 6.0 copy-start.6
  201.0 118.1 %copy-start.3 = (bf16[1024,256]{1,0:T(8,128)(2,1)S(1)}, bf16[1024,256]{1,0:T(8,128)(2,1)}, u32[]{:S(2)}) copy-start(bf16[1024,256]{1,0:T(8,128)(2,1)} %param.23) | copy-start | bytes 1572868
  770.0 4.0 copy-start.2
Sparse Core Ops, SparseCore 0:
  775.9 135.0 all-reduce.8
where the time goes:
time: 948 us; the launch traced here: 947 us
  blocking collectives  809 us (85%)
  waiting for transfers between devices  78.7 us (8%)
  matrix products  25.7 us (3%)
  between operations  15 us (2%)
  local copies, waits for them, and re-layouts  11.7 us (1%)
    psum x2, blocking collectives, shards(): lax.psum((query_part, kv_part, square_part), 'kv')  229 us
    psum x2, blocking collectives, shards(): totals, sums = lax.psum((totals * factor, sums * factor[..., None]), 'kv')  223 us
    psum x2, blocking collectives, shards(): resid = flat + lax.psum(attn_part, 'head')  164 us
    pmax x2, blocking collectives, shards(): largest = lax.pmax(running, 'kv')  112 us
    psum x1, waiting for transfers between devices, shards(): gate_sum, square_total = lax.psum((gate_up_part, square_two), 'kv')  78.7 us
    psum x1, blocking collectives, shards(): gate_sum, square_total = lax.psum((gate_up_part, square_two), 'kv')  55.7 us
    psum x1, blocking collectives, shards(): down_sum = lax.psum(down_part, 'head')  25.4 us
  transfers between devices with their start and end apart: 1, of which 1 were waited for; matrix products, arithmetic and copies ran while one was open for 0% of the time, Pallas kernels for 0%

commit v1 on v0

v1 whole, which is shorter than its diff:
```python
import functools

import jax
import jax.numpy as jnp
from jax import lax
from jax.experimental import pallas as pl
from jax.experimental.pallas import tpu as pltpu
from jax.sharding import PartitionSpec as P

D = 8192
EPSILON = 1e-05
NEGATIVE = -1e30
F32 = jnp.float32
BF16 = jnp.bfloat16
LANES = 128
VMEM = pl.BlockSpec(memory_space=pltpu.VMEM)
SMEM = pl.BlockSpec(memory_space=pltpu.SMEM)
ANY = pl.BlockSpec(memory_space=pl.ANY)


def exchange(x, axis):
    return lax.all_to_all(x, axis, 0, 0, tiled=True)


def call(body, out_shape, args, specs=None, scratch=(), limit=24):
    return pl.pallas_call(
        body,
        out_shape=out_shape,
        in_specs=[VMEM] * len(args) if specs is None else specs,
        out_specs=jax.tree.map(lambda _: VMEM, out_shape),
        scratch_shapes=list(scratch),
        compiler_params=pltpu.CompilerParams(vmem_limit_bytes=int(limit * 2**20)),
    )(*args)


def project(
    tokens_at, gain_at, w_query_at, w_kv_at, out, tokens, gain, w_query, w_kv, wide, sems
):
    copies = [
        pltpu.make_async_copy(src, dst, sems.at[i])
        for i, (src, dst) in enumerate(
            ((w_kv_at, w_kv), (tokens_at, tokens), (gain_at, gain), (w_query_at, w_query))
        )
    ]
    for copy in copies:
        copy.start()
    for copy in copies[:3]:
        copy.wait()
    rows = tokens.shape[0] * tokens.shape[1]
    width = tokens.shape[2]
    wide[...] = w_kv[...].astype(F32).reshape(2 * width, LANES)
    flat = tokens[...].astype(F32).reshape(rows, tokens.shape[2])
    normed = (flat * gain[...].astype(F32).reshape(1, -1)).astype(BF16)
    kv = [
        jnp.dot(
            normed, wide[pl.ds(i, width, stride=2), :].astype(BF16), preferred_element_type=F32
        )
        for i in range(2)
    ]
    copies[3].wait()
    q = jnp.dot(normed, w_query[...], preferred_element_type=F32)
    stat = jnp.broadcast_to(jnp.sum(flat * flat, -1, keepdims=True), (rows, LANES))
    for half in range(2):
        for slot in range(8):
            if slot < 4:
                at = (half * 4 + slot) * LANES
                part = q[:, at : at + LANES]
            elif slot == 4:
                part = kv[half]
            else:
                part = stat
            out[pl.ds(half * 8 + slot, rows, stride=16), :] = part


def finish(got, relaid, out):
    total = jnp.sum(got[...], 0)
    inv = lax.rsqrt(total[7:8] / D + EPSILON)
    out[...] = jnp.broadcast_to((total * inv).astype(BF16)[None], out.shape)


def attend(lengths, owner, index, whole, keys, values, out, stored):
    rollouts, span, hd = keys.shape
    scale = hd ** (-0.5)
    row = lax.broadcasted_iota(jnp.int32, (8, LANES), 0)
    lane = lax.broadcasted_iota(jnp.int32, (16, LANES), 1)
    column = lax.broadcasted_iota(jnp.int32, (16, span), 1)
    step = lax.broadcasted_iota(jnp.int32, (16, 1), 0) // 8
    here = index[0] == 0
    queries, news = [], []
    for b in range(rollouts):
        tiles, pairs = [], []
        for s in range(2):
            low = whole[(s * rollouts + b) * 2].astype(F32)
            high = whole[(s * rollouts + b) * 2 + 1].astype(F32)
            tiles.append(jnp.where(row < 4, low, pltpu.roll(high, 4, 0)))
            pairs.append((low[4:5], high[4:5]))
            pair = jnp.concatenate(pairs[s], 0)
            mine = owner[s] == index[0]
            stored[0, s, b, 0] = jnp.where(mine, pair, jnp.zeros_like(pair)).astype(BF16)
        queries.append(jnp.concatenate(tiles, 0))
        news.append(pairs)
    scores = []
    for b in range(rollouts):
        scores.append(
            lax.dot_general(
                queries[b].astype(BF16),
                keys[b],
                (((1,), (1,)), ((), ())),
                preferred_element_type=F32,
            )
            * scale
        )
    weights, totals, tops, extras = [], [], [], []
    for b in range(rollouts):
        keep = column < lengths[b] - index[0] * span
        masked = jnp.where(keep, scores[b], NEGATIVE)
        top = jnp.max(masked, -1, keepdims=True)
        fresh = []
        for t in range(2):
            allowed = (step >= t) & here
            score = jnp.sum(queries[b] * news[b][t][0], -1, keepdims=True) * scale
            fresh.append((allowed, jnp.where(allowed, score, NEGATIVE)))
            top = jnp.maximum(top, fresh[t][1])
        e = jnp.where(keep, jnp.exp(masked - top), 0.0)
        extra = [jnp.where(ok, jnp.exp(score - top), 0.0) for ok, score in fresh]
        totals.append(jnp.sum(e, -1, keepdims=True) + extra[0] + extra[1])
        weights.append(e.astype(BF16))
        tops.append(top)
        extras.append(extra)
    for b in range(rollouts):
        sums = jnp.dot(weights[b], values[b], preferred_element_type=F32)
        for t in range(2):
            sums = sums + extras[b][t].astype(BF16).astype(F32) * news[b][t][1]
        stat = jnp.where(lane < LANES // 2, tops[b], totals[b])
        for s in range(2):
            sums_s, stat_s = sums[s * 8 : s * 8 + 8], stat[s * 8 : s * 8 + 8]
            at = (s * rollouts + b) * 2
            out[at] = jnp.where(row < 4, sums_s, pltpu.roll(stat_s, 4, 0))
            out[at + 1] = jnp.where(row < 4, pltpu.roll(sums_s, 4, 0), stat_s)


def combine(got, out):
    tops = got[:, 4:, :1]
    factor = jnp.exp(tops - jnp.max(tops, 0, keepdims=True))
    total = jnp.sum(factor * got[:, 4:, LANES // 2 : LANES // 2 + 1], 0)
    context = jnp.sum(factor * got[:, :4, :], 0) / total
    out[...] = jnp.broadcast_to(context.astype(BF16)[None], out.shape)


def gathered_dot(used, whole, w, out, wide):
    chunks, lines = whole.shape[:2]
    wide[...] = whole[...].astype(F32).reshape(chunks * lines, LANES)
    rows = chunks // 2
    parts = [
        wide[pl.ds(half * lines + slot, rows, stride=2 * lines), :].astype(BF16)
        for half in range(2)
        for slot in range(used)
    ]
    part = jnp.dot(jnp.concatenate(parts, 1), w[...], preferred_element_type=F32)
    out[...] = jnp.broadcast_to(part[None], out.shape)


def gate_up(got, tokens, gain, w, resid_out, out):
    rows, width = resid_out.shape
    resid = tokens[...].astype(F32).reshape(rows, width) + jnp.sum(got[...], 0)
    resid_out[...] = resid
    normed = (resid * gain[...].astype(F32).reshape(1, -1)).astype(BF16)
    stat = jnp.broadcast_to(jnp.sum(resid * resid, -1, keepdims=True), (rows, LANES))
    lines = w.shape[2] // 2 // LANES
    for which in range(2):
        part = jnp.dot(normed, w[which], preferred_element_type=F32)
        for half in range(2):
            for slot in range(16):
                at = (half * lines + slot) * LANES
                out[pl.ds(half * 32 + which * 16 + slot, rows, stride=64), :] = (
                    part[:, at : at + LANES] if slot < lines else stat
                )


def activate(got, out):
    total = jnp.sum(got[...], 0)
    inv = lax.rsqrt(total[15:16] / D + EPSILON)
    gate, up = total[:16] * inv, total[16:] * inv
    hidden = (gate * jax.nn.sigmoid(gate) * up).astype(BF16)
    out[...] = jnp.broadcast_to(hidden[None], out.shape)


def close(resid, got, out):
    total = resid[...] + jnp.sum(got[...], 0)
    out[...] = total.astype(BF16).reshape(out.shape)


def shards(
    tokens,
    norm_attn,
    norm_ffn,
    w_query,
    w_kv,
    w_out,
    w_gate_up,
    w_down,
    cache_keys,
    cache_values,
    lengths,
    owner,
):
    kv_index = lax.axis_index("kv").astype(jnp.int32)
    kv_count = lax.axis_size("kv")
    head_count = lax.axis_size("head")
    steps, rollouts, width = tokens.shape
    rows = steps * rollouts
    span, hd = cache_keys.shape[2:]
    shape = jax.ShapeDtypeStruct
    w_gate_up = w_gate_up.transpose(1, 0, 2)

    chunk = call(
        project,
        shape((kv_count * 8, hd), F32),
        (tokens, norm_attn, w_query, w_kv),
        [ANY] * 4,
        [pltpu.VMEM(x.shape, x.dtype) for x in (tokens, norm_attn, w_query, w_kv)]
        + [pltpu.VMEM((2 * width, hd), F32), pltpu.SemaphoreType.DMA((4,))],
        60,
    )
    got = exchange(chunk.reshape(kv_count, 8, hd), "kv")
    mine = call(
        finish, shape((kv_count, 8, hd), BF16), (got, w_gate_up), [VMEM, ANY], limit=60
    )
    whole = exchange(mine, "kv")

    cache_shape = (rollouts, span, hd)
    keys, values = cache_keys.reshape(cache_shape), cache_values.reshape(cache_shape)
    chunk, stored = call(
        attend,
        (shape((kv_count, 8, hd), F32), shape((1, steps, rollouts, 1, 2, hd), BF16)),
        (lengths, owner, kv_index.reshape(1), whole, keys, values),
        [SMEM, SMEM, SMEM, VMEM, VMEM, VMEM],
    )
    got = exchange(chunk, "kv")
    context = exchange(call(combine, shape((kv_count, 4, hd), BF16), (got,)), "kv")
    part = call(
        functools.partial(gathered_dot, 4),
        shape((head_count, rows, width), F32),
        (context, w_out),
        scratch=[pltpu.VMEM((kv_count * 4, hd), F32)],
    )
    got = exchange(part, "head")

    resid, chunk = call(
        gate_up,
        (shape((rows, width), F32), shape((kv_count * 32, hd), F32)),
        (got, tokens, norm_ffn, w_gate_up),
    )
    got = exchange(chunk.reshape(kv_count, 32, hd), "kv")
    hidden = exchange(call(activate, shape((kv_count, 16, hd), BF16), (got,)), "kv")
    part = call(
        functools.partial(gathered_dot, w_down.shape[0] // 2 // hd),
        shape((head_count, rows, width), F32),
        (hidden, w_down),
        scratch=[pltpu.VMEM((kv_count * 16, hd), F32)],
    )
    got = exchange(part, "head")
    layer_out = call(close, shape((steps, rollouts, width), BF16), (resid, got))
    return (layer_out, stored)


def solution(mesh):
    return jax.shard_map(
        shards,
        mesh=mesh,
        in_specs=(
            P(None, None, "kv"),
            P("kv"),
            P("kv"),
            P("kv", "head"),
            P("kv", None, "head"),
            P("head", "kv"),
            P("kv", None, "head"),
            P("head", "kv"),
            P(None, "head", "kv", None),
            P(None, "head", "kv", None),
            P(),
            P(),
        ),
        out_specs=(P(None, None, "kv"), P("kv", None, None, "head", None, None)),
        check_vma=False,
    )
```

time: 948 us -> 128 us (0.14)
  blocking collectives: 809 us -> 83.4 us
  waiting for transfers between devices: 78.7 us -> 14.1 us
  matrix products: 25.7 us -> 0 us
  starting transfers between devices: 0.04 us -> 16 us
  between operations: 15 us -> 0.74 us
    psum x8 -> x0, blocking collectives: 698 us -> none  [the longest x2 229 us: shards(): lax.psum((query_part, kv_part, square_part), 'kv')]
    pmax x2 -> x0, blocking collectives: 112 us -> none  [shards(): largest = lax.pmax(running, 'kv')]
    all_to_all x0 -> x6, blocking collectives: none -> 83.4 us  [exchange(): return lax.all_to_all(x, axis, 0, 0, tiled=True)]
    psum x1 -> x0, waiting for transfers between devices: 78.7 us -> none  [shards(): gate_sum, square_total = lax.psum((gate_up_part, square_two), 'kv')]
    dot_general x21 -> x0, matrix products: 25.7 us -> none  [the longest x4 6.71 us: visit_block(): jnp.einsum('sbngd,bncd->sbngc', query, keys, preferred_element_type=jnp.f...]
    all_to_all x0 -> x2, starting transfers between devices: none -> 16 us  [exchange(): return lax.all_to_all(x, axis, 0, 0, tiled=True)]
    all_to_all x0 -> x2, waiting for transfers between devices: none -> 14.1 us  [exchange(): return lax.all_to_all(x, axis, 0, 0, tiled=True)]
  transfers between devices with their start and end apart: 1 -> 2, of which waited for: 1 -> 2; matrix products, arithmetic and copies ran while one was open for 0% -> 3% of each run, Pallas kernels for 0% -> 0%
where the time goes in v1:
time: 128 us
  blocking collectives  83.4 us (65%)
  starting transfers between devices  16 us (12%)
  waiting for transfers between devices  14.1 us (11%)
  Pallas kernels  7.2 us (6%)
  local copies, waits for them, and re-layouts  6.45 us (5%)
    all_to_all x6, blocking collectives, exchange(): return lax.all_to_all(x, axis, 0, 0, tiled=True)  83.4 us
    all_to_all x2, starting transfers between devices, exchange(): return lax.all_to_all(x, axis, 0, 0, tiled=True)  16 us
    all_to_all x2, waiting for transfers between devices, exchange(): return lax.all_to_all(x, axis, 0, 0, tiled=True)  14.1 us
    pallas_call x9, Pallas kernels, call(): pl.pallas_call(body, out_shape=out_shape, in_specs=[VMEM] * len(args) if...  7.2 us
    unnamed x21, local copies, waits for them, and re-layouts  6.45 us
  transfers between devices with their start and end apart: 2, of which 2 were waited for; matrix products, arithmetic and copies ran while one was open for 3% of the time, Pallas kernels for 0%

profile of v1, /device:TPU:1, one launch (start us, length us, event | category | flops | bytes accessed | tf_op | source)
XLA Modules:
  0.0 127.8 jit_solution(10176978935487434250)
XLA Ops:
  0.6 2.0 %shard_map.131 = f32[256,128]{1,0:T(8,128)} custom-call(bf16[2,8,256]{2,1,0:T(8,128)(2,1)} %tokens.1, bf16[256]{0:T(256)(128)(2,1)} %gain_at.1, bf16[256,1024]{1,0:T(8,128)(2,1)} %w_query_at.1, bf16[256,2,128]{2,1,0:T(2,128)(2,1)} %w_kv_at.1), custom_call_target="tpu_custom_call" | custom-call | tf_op jit(solution)/shard_map/pallas_call | solution.py:26
  2.7 11.9 %all-to-all-start = ((f32[32,8,128]{2,1,0:T(8,128)}), f32[32,8,128]{2,1,0:T(8,128)S(1)}, u32[]{:S(2)}, u32[]{:S(2)}) async-start(f32[32,8,128]{2,1,0:T(8,128)} %bitcast.13), calls=%async_computation | async-start | bytes 262144 | tf_op jit(solution)/shard_map/all_to_all | solution.py:22
  14.5 4.2 %copy.16 = bf16[256,2,3584]{2,0,1:T(8,128)(2,1)} copy(bf16[256,2,3584]{2,1,0:T(2,128)(2,1)} %param.18) | data formatting | bytes 7340032 | tf_op args[6]
  18.7 5.1 %all-to-all-done.got = f32[32,8,128]{2,1,0:T(8,128)S(1)} async-done(((f32[32,8,128]{2,1,0:T(8,128)}), f32[32,8,128]{2,1,0:T(8,128)S(1)}, u32[]{:S(2)}, u32[]{:S(2)}) %all-to-all-start) | async-done | bytes 131104 | tf_op jit(solution)/shard_map/all_to_all | solution.py:22
  23.9 0.6 copy-done.9
  24.5 1.6 %shard_map.132 = bf16[32,8,128]{2,1,0:T(8,128)(2,1)} custom-call(f32[32,8,128]{2,1,0:T(8,128)} %copy-done.9, bf16[2,256,3584]{2,1,0:T(8,128)(2,1)} %bitcast.8), custom_call_target="tpu_custom_call" | custom-call | tf_op jit(solution)/shard_map/pallas_call | solution.py:26
  26.1 4.1 %all-to-all-start.1 = ((bf16[32,8,128]{2,1,0:T(8,128)(2,1)}), bf16[32,8,128]{2,1,0:T(8,128)(2,1)S(1)}, u32[]{:S(2)}, u32[]{:S(2)}) async-start(bf16[32,8,128]{2,1,0:T(8,128)(2,1)} %shard_map.132), calls=%async_computation.1 | async-start | bytes 131072 | tf_op jit(solution)/shard_map/all_to_all | solution.py:22
  30.2 8.9 %all-to-all-done.1.whole = bf16[32,8,128]{2,1,0:T(8,128)(2,1)S(1)} async-done(((bf16[32,8,128]{2,1,0:T(8,128)(2,1)}), bf16[32,8,128]{2,1,0:T(8,128)(2,1)S(1)}, u32[]{:S(2)}, u32[]{:S(2)}) %all-to-all-start.1) | async-done | bytes 65568 | tf_op jit(solution)/shard_map/all_to_all | solution.py:22
  39.2 0.0 copy-done.1
  39.2 0.0 copy-done.6
  39.2 0.0 copy-done.7
  39.2 0.0 copy-start.2
  39.2 1.6 %copy-done.2 = bf16[8,1,1024,128]{3,2,1,0:T(8,128)(2,1)S(1)} copy-done((bf16[8,1,1024,128]{3,2,1,0:T(8,128)(2,1)S(1)}, bf16[8,1,1024,128]{3,2,1,0:T(8,128)(2,1)}, u32[]{:S(2)}) %copy-start.2) | copy-done | bytes 2097176
  40.8 1.6 %shard_map.133 = (f32[32,8,128]{2,1,0:T(8,128)S(1)}, bf16[1,2,8,1,2,128]{5,4,3,2,1,0:T(2,128)(2,1)}) custom-call(s32[8]{0:T(128)S(1)} %copy-done.6, s32[2]{0:T(128)S(1)} %copy-done.7, s32[1]{0:T(128)} %bitcast.index, bf16[32,8,128]{2,1,0:T(8,128)(2,1)S(1)} %all-to-all-done.1.whole, bf16[8,1024,128]{2,1,0:T(8,128)(2,1)S(1)} %bitcast.10, ...), custom_call_target="tpu_custom_call" | custom-call | tf_op jit(solution)/shard_map/pallas_call | solution.py:26
  42.4 12.4 %all_to_all.40.got = f32[32,8,128]{2,1,0:T(8,128)S(1)} all-to-all(f32[32,8,128]{2,1,0:T(8,128)S(1)} %get-tuple-element.6), channel_id=1, replica_groups=mesh['kv'=32,'head'=8] {'kv'}, dimensions={0} | all-to-all | bytes 262144 | tf_op jit(solution)/shard_map/all_to_all | solution.py:22
  54.7 0.2 shard_map.134
  54.9 11.9 %all_to_all.41.whole = bf16[32,4,128]{2,1,0:T(4,128)(2,1)S(1)} all-to-all(bf16[32,4,128]{2,1,0:T(4,128)(2,1)S(1)} %shard_map.134), channel_id=1, replica_groups=mesh['kv'=32,'head'=8] {'kv'}, dimensions={0} | all-to-all | bytes 65536 | tf_op jit(solution)/shard_map/all_to_all | solution.py:22
  66.8 0.0 copy-done.4
  66.8 0.2 shard_map.135
  67.0 14.7 %all_to_all.42.got = f32[8,16,256]{2,1,0:T(8,128)S(1)} all-to-all(f32[8,16,256]{2,1,0:T(8,128)S(1)} %shard_map.135), channel_id=1, replica_groups=mesh['kv'=32,'head'=8] {'head'}, dimensions={0} | all-to-all | bytes 262144 | tf_op jit(solution)/shard_map/all_to_all | solution.py:22
  81.8 0.0 copy-done
  81.8 0.0 copy-done.5
  81.8 0.0 copy-done.8
  81.8 0.0 copy-start.3
  81.8 0.6 shard_map.136
  82.4 19.1 %all_to_all.43.got = f32[32,32,128]{2,1,0:T(8,128)S(1)} all-to-all(f32[32,32,128]{2,1,0:T(8,128)S(1)} %bitcast.12), channel_id=1, replica_groups=mesh['kv'=32,'head'=8] {'kv'}, dimensions={0} | all-to-all | bytes 1048576 | tf_op jit(solution)/shard_map/all_to_all | solution.py:22
  101.5 0.1 shard_map.137
  101.6 14.4 %all_to_all.44.whole = bf16[32,16,128]{2,1,0:T(8,128)(2,1)S(1)} all-to-all(bf16[32,16,128]{2,1,0:T(8,128)(2,1)S(1)} %shard_map.137), channel_id=1, replica_groups=mesh['kv'=32,'head'=8] {'kv'}, dimensions={0} | all-to-all | bytes 262144 | tf_op jit(solution)/shard_map/all_to_all | solution.py:22
  116.0 0.0 copy-done.3
  116.0 0.4 shard_map.138
  116.4 10.8 %all_to_all.45.got = f32[8,16,256]{2,1,0:T(8,128)S(1)} all-to-all(f32[8,16,256]{2,1,0:T(8,128)S(1)} %shard_map.138), channel_id=1, replica_groups=mesh['kv'=32,'head'=8] {'head'}, dimensions={0} | all-to-all | bytes 262144 | tf_op jit(solution)/shard_map/all_to_all | solution.py:22
  127.2 0.6 shard_map.139
  (8 shorter events, 0.0 us)
Async XLA Ops:
  2.7 21.2 %all-to-all-start = ((f32[32,8,128]{2,1,0:T(8,128)}), f32[32,8,128]{2,1,0:T(8,128)S(1)}, u32[]{:S(2)}, u32[]{:S(2)}) async-start(f32[32,8,128]{2,1,0:T(8,128)} %bitcast.13), calls=%async_computation | async-start | bytes 262144 | tf_op jit(solution)/shard_map/all_to_all | solution.py:22
  18.7 20.4 %copy-start.1 = (bf16[8,1,1024,128]{3,2,1,0:T(8,128)(2,1)S(1)}, bf16[8,1,1024,128]{3,2,1,0:T(8,128)(2,1)}, u32[]{:S(2)}) copy-start(bf16[8,1,1024,128]{3,2,1,0:T(8,128)(2,1)} %param.20) | copy-start | bytes 6291460
  18.7 20.4 %copy-start.6 = (s32[8]{0:T(128)S(1)}, s32[8]{0:T(128)}, u32[]{:S(2)}) copy-start(s32[8]{0:T(128)} %lengths.1) | copy-start | bytes 100
  18.7 20.4 %copy-start.7 = (s32[2]{0:T(128)S(1)}, s32[2]{0:T(128)}, u32[]{:S(2)}) copy-start(s32[2]{0:T(128)} %owner.1) | copy-start | bytes 28
  23.9 0.6 copy-start.9
  26.1 13.1 %all-to-all-start.1 = ((bf16[32,8,128]{2,1,0:T(8,128)(2,1)}), bf16[32,8,128]{2,1,0:T(8,128)(2,1)S(1)}, u32[]{:S(2)}, u32[]{:S(2)}) async-start(bf16[32,8,128]{2,1,0:T(8,128)(2,1)} %shard_map.132), calls=%async_computation.1 | async-start | bytes 131072 | tf_op jit(solution)/shard_map/all_to_all | solution.py:22
  39.2 1.6 %copy-start.2 = (bf16[8,1,1024,128]{3,2,1,0:T(8,128)(2,1)S(1)}, bf16[8,1,1024,128]{3,2,1,0:T(8,128)(2,1)}, u32[]{:S(2)}) copy-start(bf16[8,1,1024,128]{3,2,1,0:T(8,128)(2,1)} %param.21) | copy-start | bytes 6291460
  40.8 26.1 %copy-start.4 = (bf16[1024,256]{1,0:T(8,128)(2,1)S(1)}, bf16[1024,256]{1,0:T(8,128)(2,1)}, u32[]{:S(2)}) copy-start(bf16[1024,256]{1,0:T(8,128)(2,1)} %w.2) | copy-start | bytes 1572868
  40.8 41.0 %copy-start = (bf16[256,2,3584]{2,0,1:T(8,128)(2,1)S(1)}, bf16[256,2,3584]{2,0,1:T(8,128)(2,1)}, u32[]{:S(2)}) copy-start(bf16[256,2,3584]{2,0,1:T(8,128)(2,1)} %copy.16) | copy-start | bytes 11010052
  40.8 41.0 %copy-start.5 = (bf16[2,8,256]{2,1,0:T(8,128)(2,1)S(1)}, bf16[2,8,256]{2,1,0:T(8,128)(2,1)}, u32[]{:S(2)}) copy-start(bf16[2,8,256]{2,1,0:T(8,128)(2,1)} %tokens.1) | copy-start | bytes 24580
  40.8 41.0 %copy-start.8 = (bf16[256]{0:T(256)(128)(2,1)S(1)}, bf16[256]{0:T(256)(128)(2,1)}, u32[]{:S(2)}) copy-start(bf16[256]{0:T(256)(128)(2,1)} %gain.1) | copy-start | bytes 1540
  81.8 34.3 %copy-start.3 = (bf16[3584,256]{1,0:T(8,128)(2,1)S(1)}, bf16[3584,256]{1,0:T(8,128)(2,1)}, u32[]{:S(2)}) copy-start(bf16[3584,256]{1,0:T(8,128)(2,1)} %w.3) | copy-start | bytes 5505028

commit v2 on v1

--- a/solution.py
+++ b/solution.py
@@ -13,6 +13,7 @@
 F32 = jnp.float32
 BF16 = jnp.bfloat16
 LANES = 128
+TOP = 32767.0
 VMEM = pl.BlockSpec(memory_space=pltpu.VMEM)
 SMEM = pl.BlockSpec(memory_space=pltpu.SMEM)
 ANY = pl.BlockSpec(memory_space=pl.ANY)
@@ -34,7 +35,7 @@
 
 
 def project(
-    tokens_at, gain_at, w_query_at, w_kv_at, out, tokens, gain, w_query, w_kv, wide, sems
+    index, tokens_at, gain_at, w_query_at, w_kv_at, out, tokens, gain, w_query, w_kv, wide, sems
 ):
     copies = [
         pltpu.make_async_copy(src, dst, sems.at[i])
@@ -72,7 +73,11 @@
             out[pl.ds(half * 8 + slot, rows, stride=16), :] = part
 
 
-def finish(got, relaid, out):
+def anchor(relaid, out):
+    out[0] = 0
+
+
+def finish(got, token, values, out):
     total = jnp.sum(got[...], 0)
     inv = lax.rsqrt(total[7:8] / D + EPSILON)
     out[...] = jnp.broadcast_to((total * inv).astype(BF16)[None], out.shape)
@@ -160,26 +165,47 @@
     out[...] = jnp.broadcast_to(part[None], out.shape)
 
 
-def gate_up(got, tokens, gain, w, resid_out, out):
+def exponent(x):
+    return jnp.ceil(jnp.log2(jnp.maximum(x, 1e-30)))
+
+
+def gate_up(got, tokens, gain, w, resid_out, out, wide):
     rows, width = resid_out.shape
     resid = tokens[...].astype(F32).reshape(rows, width) + jnp.sum(got[...], 0)
     resid_out[...] = resid
     normed = (resid * gain[...].astype(F32).reshape(1, -1)).astype(BF16)
-    stat = jnp.broadcast_to(jnp.sum(resid * resid, -1, keepdims=True), (rows, LANES))
+    stat = jnp.sum(resid * resid, -1, keepdims=True)
+    power = exponent(stat)
+    scaled = stat * jnp.exp2(-power) * TOP
+    high = jnp.floor(scaled)
+    low = jnp.floor((scaled - high) * TOP)
     lines = w.shape[2] // 2 // LANES
-    for which in range(2):
-        part = jnp.dot(normed, w[which], preferred_element_type=F32)
-        for half in range(2):
+    across = lines * LANES
+    parts = [jnp.dot(normed, w[which], preferred_element_type=F32) for which in range(2)]
+    for half in range(2):
+        pair = [part[:, half * across : (half + 1) * across] for part in parts]
+        size = jnp.maximum(*(jnp.max(jnp.abs(part), -1, keepdims=True) for part in pair))
+        shift = exponent(size)
+        factor = jnp.exp2(-shift) * TOP
+        extras = ((shift, high), (low, power))
+        for which in range(2):
             for slot in range(16):
-                at = (half * lines + slot) * LANES
-                out[pl.ds(half * 32 + which * 16 + slot, rows, stride=64), :] = (
-                    part[:, at : at + LANES] if slot < lines else stat
-                )
+                if slot < lines:
+                    line = jnp.floor(
+                        pair[which][:, slot * LANES : (slot + 1) * LANES] * factor + 0.5
+                    )
+                    line = jnp.clip(line, -TOP, TOP)
+                else:
+                    line = jnp.broadcast_to(extras[which][slot - lines], (rows, LANES))
+                wide[pl.ds(half * 32 + which * 16 + slot, rows, stride=64), :] = line
+    out[...] = wide[...].astype(jnp.int32).astype(jnp.int16).reshape(out.shape)
 
 
 def activate(got, out):
-    total = jnp.sum(got[...], 0)
-    inv = lax.rsqrt(total[15:16] / D + EPSILON)
+    coded = got[...].astype(jnp.int32).astype(F32)
+    total = jnp.sum(coded * (jnp.exp2(coded[:, 14:15]) / TOP), 0)
+    stats = (coded[:, 15:16] + coded[:, 30:31] / TOP) * (jnp.exp2(coded[:, 31:32]) / TOP)
+    inv = lax.rsqrt(jnp.sum(stats, 0) / D + EPSILON)
     gate, up = total[:16] * inv, total[16:] * inv
     hidden = (gate * jax.nn.sigmoid(gate) * up).astype(BF16)
     out[...] = jnp.broadcast_to(hidden[None], out.shape)
@@ -216,20 +242,27 @@
     chunk = call(
         project,
         shape((kv_count * 8, hd), F32),
-        (tokens, norm_attn, w_query, w_kv),
-        [ANY] * 4,
+        (kv_index.reshape(1), tokens, norm_attn, w_query, w_kv),
+        [SMEM] + [ANY] * 4,
         [pltpu.VMEM(x.shape, x.dtype) for x in (tokens, norm_attn, w_query, w_kv)]
         + [pltpu.VMEM((2 * width, hd), F32), pltpu.SemaphoreType.DMA((4,))],
         60,
     )
     got = exchange(chunk.reshape(kv_count, 8, hd), "kv")
-    mine = call(
-        finish, shape((kv_count, 8, hd), BF16), (got, w_gate_up), [VMEM, ANY], limit=60
-    )
-    whole = exchange(mine, "kv")
-
+    token = pl.pallas_call(
+        anchor,
+        out_shape=shape((1,), jnp.int32),
+        in_specs=[ANY],
+        out_specs=SMEM,
+        compiler_params=pltpu.CompilerParams(vmem_limit_bytes=61 * 2**20),
+    )(w_gate_up)
     cache_shape = (rollouts, span, hd)
     keys, values = cache_keys.reshape(cache_shape), cache_values.reshape(cache_shape)
+    mine = call(
+        finish, shape((kv_count, 8, hd), BF16), (got, token, values), [VMEM, SMEM, VMEM]
+    )
+    whole = exchange(mine, "kv")
+
     chunk, stored = call(
         attend,
         (shape((kv_count, 8, hd), F32), shape((1, steps, rollouts, 1, 2, hd), BF16)),
@@ -248,10 +281,11 @@
 
     resid, chunk = call(
         gate_up,
-        (shape((rows, width), F32), shape((kv_count * 32, hd), F32)),
+        (shape((rows, width), F32), shape((kv_count, 32, hd), jnp.int16)),
         (got, tokens, norm_ffn, w_gate_up),
-    )
-    got = exchange(chunk.reshape(kv_count, 32, hd), "kv")
+        scratch=[pltpu.VMEM((kv_count * 32, hd), F32)],
+    )
+    got = exchange(chunk, "kv")
     hidden = exchange(call(activate, shape((kv_count, 16, hd), BF16), (got,)), "kv")
     part = call(
         functools.partial(gathered_dot, w_down.shape[0] // 2 // hd),

time: 128 us -> 121 us (0.945)
  waiting for transfers between devices: 14.1 us -> 4.6 us
  blocking collectives: 83.4 us -> 91.7 us
  starting transfers between devices: 16 us -> 11.9 us
  local copies, waits for them, and re-layouts: 6.45 us -> 4.24 us
    all_to_all x2 -> x1, waiting for transfers between devices: 14.1 us -> 4.6 us  [exchange(): return lax.all_to_all(x, axis, 0, 0, tiled=True)]
    all_to_all x6 -> x7, blocking collectives: 83.4 us -> 91.7 us  [exchange(): return lax.all_to_all(x, axis, 0, 0, tiled=True)]
    all_to_all x2 -> x1, starting transfers between devices: 16 us -> 11.9 us  [exchange(): return lax.all_to_all(x, axis, 0, 0, tiled=True)]
    unnamed x21 -> x19, local copies, waits for them, and re-layouts: 6.45 us -> 4.24 us
  transfers between devices with their start and end apart: 2 -> 1, of which waited for: 2 -> 1; matrix products, arithmetic and copies ran while one was open for 3% -> 3% of each run, Pallas kernels for 0% -> 0%
where the time goes in v2:
time: 121 us
  blocking collectives  91.7 us (76%)
  starting transfers between devices  11.9 us (10%)
  Pallas kernels  7.53 us (6%)
  waiting for transfers between devices  4.6 us (4%)
  local copies, waits for them, and re-layouts  4.24 us (4%)
    all_to_all x7, blocking collectives, exchange(): return lax.all_to_all(x, axis, 0, 0, tiled=True)  91.7 us
    all_to_all x1, starting transfers between devices, exchange(): return lax.all_to_all(x, axis, 0, 0, tiled=True)  11.9 us
    pallas_call x9, Pallas kernels, call(): pl.pallas_call(body, out_shape=out_shape, in_specs=[VMEM] * len(args) if...  7.01 us
    all_to_all x1, waiting for transfers between devices, exchange(): return lax.all_to_all(x, axis, 0, 0, tiled=True)  4.6 us
    unnamed x19, local copies, waits for them, and re-layouts  4.24 us
  transfers between devices with their start and end apart: 1, of which 1 were waited for; matrix products, arithmetic and copies ran while one was open for 3% of the time, Pallas kernels for 0%

profile of v2, /device:TPU:1, one launch (start us, length us, event | category | flops | bytes accessed | tf_op | source)
XLA Modules:
  0.0 120.7 jit_solution(17335218923101020878)
XLA Ops:
  0.6 2.0 %shard_map.131 = f32[256,128]{1,0:T(8,128)} custom-call(s32[1]{0:T(128)} %bitcast.index, bf16[2,8,256]{2,1,0:T(8,128)(2,1)} %tokens.1, bf16[256]{0:T(256)(128)(2,1)} %gain_at.1, bf16[256,1024]{1,0:T(8,128)(2,1)} %w_query_at.1, bf16[256,2,128]{2,1,0:T(2,128)(2,1)} %w_kv_at.1), custom_call_target="tpu_custom_call" | custom-call | tf_op jit(solution)/shard_map/pallas_call | solution.py:27
  2.7 11.9 %all-to-all-start = ((f32[32,8,128]{2,1,0:T(8,128)}), f32[32,8,128]{2,1,0:T(8,128)S(1)}, u32[]{:S(2)}, u32[]{:S(2)}) async-start(f32[32,8,128]{2,1,0:T(8,128)} %bitcast.12), calls=%async_computation | async-start | bytes 262144 | tf_op jit(solution)/shard_map/all_to_all | solution.py:23
  14.6 4.2 %copy.16 = bf16[256,2,3584]{2,0,1:T(8,128)(2,1)} copy(bf16[256,2,3584]{2,1,0:T(2,128)(2,1)} %param.18) | data formatting | bytes 7340032 | tf_op args[6]
  18.7 0.5 shard_map.132.token
  19.3 0.0 copy-start.6
  19.3 0.0 copy-start.7
  19.3 4.6 %all-to-all-done.got = f32[32,8,128]{2,1,0:T(8,128)S(1)} async-done(((f32[32,8,128]{2,1,0:T(8,128)}), f32[32,8,128]{2,1,0:T(8,128)S(1)}, u32[]{:S(2)}, u32[]{:S(2)}) %all-to-all-start) | async-done | bytes 131104 | tf_op jit(solution)/shard_map/all_to_all | solution.py:23
  23.9 0.0 copy-done.1
  23.9 0.8 shard_map.133
  24.7 14.1 %all_to_all.40.whole = bf16[32,8,128]{2,1,0:T(8,128)(2,1)S(1)} all-to-all(bf16[32,8,128]{2,1,0:T(8,128)(2,1)S(1)} %shard_map.133), channel_id=1, replica_groups=mesh['kv'=32,'head'=8] {'kv'}, dimensions={0} | all-to-all | bytes 131072 | tf_op jit(solution)/shard_map/all_to_all | solution.py:23
  38.9 0.0 copy-done.6
  38.9 0.0 copy-done.7
  38.9 0.0 copy-done.2
  38.9 0.0 copy-start.4
  38.9 0.0 copy-start.5
  38.9 0.0 copy-start.8
  38.9 1.6 %shard_map.134 = (f32[32,8,128]{2,1,0:T(8,128)S(1)}, bf16[1,2,8,1,2,128]{5,4,3,2,1,0:T(2,128)(2,1)}) custom-call(s32[8]{0:T(128)S(1)} %copy-done.6, s32[2]{0:T(128)S(1)} %copy-done.7, s32[1]{0:T(128)} %bitcast.index, bf16[32,8,128]{2,1,0:T(8,128)(2,1)S(1)} %all_to_all.40.whole, bf16[8,1024,128]{2,1,0:T(8,128)(2,1)S(1)} %bitcast.11, ...), custom_call_target="tpu_custom_call" | custom-call | tf_op jit(solution)/shard_map/pallas_call | solution.py:27
  40.5 12.5 %all_to_all.41.got = f32[32,8,128]{2,1,0:T(8,128)S(1)} all-to-all(f32[32,8,128]{2,1,0:T(8,128)S(1)} %get-tuple-element.6), channel_id=1, replica_groups=mesh['kv'=32,'head'=8] {'kv'}, dimensions={0} | all-to-all | bytes 262144 | tf_op jit(solution)/shard_map/all_to_all | solution.py:23
  53.0 0.2 shard_map.135
  53.2 12.0 %all_to_all.42.whole = bf16[32,4,128]{2,1,0:T(4,128)(2,1)S(1)} all-to-all(bf16[32,4,128]{2,1,0:T(4,128)(2,1)S(1)} %shard_map.135), channel_id=1, replica_groups=mesh['kv'=32,'head'=8] {'kv'}, dimensions={0} | all-to-all | bytes 65536 | tf_op jit(solution)/shard_map/all_to_all | solution.py:23
  65.2 0.2 shard_map.136
  65.4 14.4 %all_to_all.43.got = f32[8,16,256]{2,1,0:T(8,128)S(1)} all-to-all(f32[8,16,256]{2,1,0:T(8,128)S(1)} %shard_map.136), channel_id=1, replica_groups=mesh['kv'=32,'head'=8] {'head'}, dimensions={0} | all-to-all | bytes 262144 | tf_op jit(solution)/shard_map/all_to_all | solution.py:23
  79.8 0.0 copy-done.5
  79.8 0.0 copy-start.3
  79.8 1.0 shard_map.137
  80.8 14.1 %all_to_all.44.got = s16[32,32,128]{2,1,0:T(8,128)(2,1)S(1)} all-to-all(s16[32,32,128]{2,1,0:T(8,128)(2,1)S(1)} %get-tuple-element.8), channel_id=1, replica_groups=mesh['kv'=32,'head'=8] {'kv'}, dimensions={0} | all-to-all | bytes 524288 | tf_op jit(solution)/shard_map/all_to_all | solution.py:23
  95.0 0.1 shard_map.138
  95.1 13.9 %all_to_all.45.whole = bf16[32,16,128]{2,1,0:T(8,128)(2,1)S(1)} all-to-all(bf16[32,16,128]{2,1,0:T(8,128)(2,1)S(1)} %shard_map.138), channel_id=1, replica_groups=mesh['kv'=32,'head'=8] {'kv'}, dimensions={0} | all-to-all | bytes 262144 | tf_op jit(solution)/shard_map/all_to_all | solution.py:23
  109.0 0.0 copy-done.3
  109.0 0.4 shard_map.139
  109.4 10.7 %all_to_all.46.got = f32[8,16,256]{2,1,0:T(8,128)S(1)} all-to-all(f32[8,16,256]{2,1,0:T(8,128)S(1)} %shard_map.139), channel_id=1, replica_groups=mesh['kv'=32,'head'=8] {'head'}, dimensions={0} | all-to-all | bytes 262144 | tf_op jit(solution)/shard_map/all_to_all | solution.py:23
  120.1 0.6 shard_map.140
  (6 shorter events, 0.0 us)
Async XLA Ops:
  2.7 21.2 %all-to-all-start = ((f32[32,8,128]{2,1,0:T(8,128)}), f32[32,8,128]{2,1,0:T(8,128)S(1)}, u32[]{:S(2)}, u32[]{:S(2)}) async-start(f32[32,8,128]{2,1,0:T(8,128)} %bitcast.12), calls=%async_computation | async-start | bytes 262144 | tf_op jit(solution)/shard_map/all_to_all | solution.py:23
  18.7 5.2 %copy-start.1 = (bf16[8,1,1024,128]{3,2,1,0:T(8,128)(2,1)S(1)}, bf16[8,1,1024,128]{3,2,1,0:T(8,128)(2,1)}, u32[]{:S(2)}) copy-start(bf16[8,1,1024,128]{3,2,1,0:T(8,128)(2,1)} %param.21) | copy-start | bytes 6291460
  19.3 19.6 %copy-start.6 = (s32[8]{0:T(128)S(1)}, s32[8]{0:T(128)}, u32[]{:S(2)}) copy-start(s32[8]{0:T(128)} %lengths.1) | copy-start | bytes 100
  19.3 19.6 %copy-start.7 = (s32[2]{0:T(128)S(1)}, s32[2]{0:T(128)}, u32[]{:S(2)}) copy-start(s32[2]{0:T(128)} %owner.1) | copy-start | bytes 28
  23.9 15.0 %copy-start.2 = (bf16[8,1,1024,128]{3,2,1,0:T(8,128)(2,1)S(1)}, bf16[8,1,1024,128]{3,2,1,0:T(8,128)(2,1)}, u32[]{:S(2)}) copy-start(bf16[8,1,1024,128]{3,2,1,0:T(8,128)(2,1)} %param.20) | copy-start | bytes 6291460
  38.9 26.3 %copy-start.4 = (bf16[1024,256]{1,0:T(8,128)(2,1)S(1)}, bf16[1024,256]{1,0:T(8,128)(2,1)}, u32[]{:S(2)}) copy-start(bf16[1024,256]{1,0:T(8,128)(2,1)} %w.2) | copy-start | bytes 1572868
  38.9 40.9 %copy-start = (bf16[256,2,3584]{2,0,1:T(8,128)(2,1)S(1)}, bf16[256,2,3584]{2,0,1:T(8,128)(2,1)}, u32[]{:S(2)}) copy-start(bf16[256,2,3584]{2,0,1:T(8,128)(2,1)} %copy.16) | copy-start | bytes 11010052
  38.9 40.9 %copy-start.5 = (bf16[2,8,256]{2,1,0:T(8,128)(2,1)S(1)}, bf16[2,8,256]{2,1,0:T(8,128)(2,1)}, u32[]{:S(2)}) copy-start(bf16[2,8,256]{2,1,0:T(8,128)(2,1)} %tokens.1) | copy-start | bytes 24580
  38.9 40.9 %copy-start.8 = (bf16[256]{0:T(256)(128)(2,1)S(1)}, bf16[256]{0:T(256)(128)(2,1)}, u32[]{:S(2)}) copy-start(bf16[256]{0:T(256)(128)(2,1)} %gain.1) | copy-start | bytes 1540
  79.8 29.2 %copy-start.3 = (bf16[3584,256]{1,0:T(8,128)(2,1)S(1)}, bf16[3584,256]{1,0:T(8,128)(2,1)}, u32[]{:S(2)}) copy-start(bf16[3584,256]{1,0:T(8,128)(2,1)} %w.3) | copy-start | bytes 5505028

commit v3 on v2

--- a/solution.py
+++ b/solution.py
@@ -15,12 +15,23 @@
 LANES = 128
 TOP = 32767.0
 VMEM = pl.BlockSpec(memory_space=pltpu.VMEM)
-SMEM = pl.BlockSpec(memory_space=pltpu.SMEM)
 ANY = pl.BlockSpec(memory_space=pl.ANY)
 
 
+def ring(sizes, first):
+    major, minor = sizes
+    return [
+        (a + first[0]) % major * minor + (b + first[1]) % minor
+        for a in range(major)
+        for b in range(minor)
+    ]
+
+
+ORDER = {"kv": ring((8, 4), (4, 2)), "head": ring((4, 2), (2, 0))}
+
+
 def exchange(x, axis):
-    return lax.all_to_all(x, axis, 0, 0, tiled=True)
+    return lax.all_to_all(x, axis, 0, 0, tiled=True, axis_index_groups=[ORDER[axis]])
 
 
 def call(body, out_shape, args, specs=None, scratch=(), limit=24):
@@ -35,7 +46,7 @@
 
 
 def project(
-    index, tokens_at, gain_at, w_query_at, w_kv_at, out, tokens, gain, w_query, w_kv, wide, sems
+    tokens_at, gain_at, w_query_at, w_kv_at, out, tokens, gain, w_query, w_kv, wide, sems
 ):
     copies = [
         pltpu.make_async_copy(src, dst, sems.at[i])
@@ -73,24 +84,23 @@
             out[pl.ds(half * 8 + slot, rows, stride=16), :] = part
 
 
-def anchor(relaid, out):
-    out[0] = 0
-
-
-def finish(got, token, values, out):
+def finish(got, relaid, values, out):
     total = jnp.sum(got[...], 0)
     inv = lax.rsqrt(total[7:8] / D + EPSILON)
     out[...] = jnp.broadcast_to((total * inv).astype(BF16)[None], out.shape)
 
 
-def attend(lengths, owner, index, whole, keys, values, out, stored):
+def attend(lengths, owner, whole, keys, values, out, stored):
     rollouts, span, hd = keys.shape
+    index = lax.axis_index("kv")
+    live = lengths[...].reshape(1, rollouts) - index * span
+    holder = owner[...].reshape(1, 2) == index
     scale = hd ** (-0.5)
     row = lax.broadcasted_iota(jnp.int32, (8, LANES), 0)
     lane = lax.broadcasted_iota(jnp.int32, (16, LANES), 1)
     column = lax.broadcasted_iota(jnp.int32, (16, span), 1)
     step = lax.broadcasted_iota(jnp.int32, (16, 1), 0) // 8
-    here = index[0] == 0
+    here = index == 0
     queries, news = [], []
     for b in range(rollouts):
         tiles, pairs = [], []
@@ -100,7 +110,7 @@
             tiles.append(jnp.where(row < 4, low, pltpu.roll(high, 4, 0)))
             pairs.append((low[4:5], high[4:5]))
             pair = jnp.concatenate(pairs[s], 0)
-            mine = owner[s] == index[0]
+            mine = holder[:, s : s + 1]
             stored[0, s, b, 0] = jnp.where(mine, pair, jnp.zeros_like(pair)).astype(BF16)
         queries.append(jnp.concatenate(tiles, 0))
         news.append(pairs)
@@ -117,7 +127,7 @@
         )
     weights, totals, tops, extras = [], [], [], []
     for b in range(rollouts):
-        keep = column < lengths[b] - index[0] * span
+        keep = column < live[:, b : b + 1]
         masked = jnp.where(keep, scores[b], NEGATIVE)
         top = jnp.max(masked, -1, keepdims=True)
         fresh = []
@@ -230,7 +240,6 @@
     lengths,
     owner,
 ):
-    kv_index = lax.axis_index("kv").astype(jnp.int32)
     kv_count = lax.axis_size("kv")
     head_count = lax.axis_size("head")
     steps, rollouts, width = tokens.shape
@@ -242,32 +251,29 @@
     chunk = call(
         project,
         shape((kv_count * 8, hd), F32),
-        (kv_index.reshape(1), tokens, norm_attn, w_query, w_kv),
-        [SMEM] + [ANY] * 4,
+        (tokens, norm_attn, w_query, w_kv),
+        [ANY] * 4,
         [pltpu.VMEM(x.shape, x.dtype) for x in (tokens, norm_attn, w_query, w_kv)]
         + [pltpu.VMEM((2 * width, hd), F32), pltpu.SemaphoreType.DMA((4,))],
         60,
     )
     got = exchange(chunk.reshape(kv_count, 8, hd), "kv")
-    token = pl.pallas_call(
-        anchor,
-        out_shape=shape((1,), jnp.int32),
-        in_specs=[ANY],
-        out_specs=SMEM,
-        compiler_params=pltpu.CompilerParams(vmem_limit_bytes=61 * 2**20),
-    )(w_gate_up)
     cache_shape = (rollouts, span, hd)
     keys, values = cache_keys.reshape(cache_shape), cache_values.reshape(cache_shape)
     mine = call(
-        finish, shape((kv_count, 8, hd), BF16), (got, token, values), [VMEM, SMEM, VMEM]
+        finish,
+        shape((kv_count, 8, hd), BF16),
+        (got, w_gate_up, values),
+        [VMEM, ANY, VMEM],
+        limit=51,
     )
     whole = exchange(mine, "kv")
 
     chunk, stored = call(
         attend,
         (shape((kv_count, 8, hd), F32), shape((1, steps, rollouts, 1, 2, hd), BF16)),
-        (lengths, owner, kv_index.reshape(1), whole, keys, values),
-        [SMEM, SMEM, SMEM, VMEM, VMEM, VMEM],
+        (lengths, owner, whole, keys, values),
+        [VMEM] * 5,
     )
     got = exchange(chunk, "kv")
     context = exchange(call(combine, shape((kv_count, 4, hd), BF16), (got,)), "kv")

time: 121 us -> 113 us (0.934)
  blocking collectives: 91.7 us -> 87 us
  waiting for transfers between devices: 4.6 us -> 0.01 us
  starting transfers between devices: 11.9 us -> 13.9 us
  Pallas kernels: 7.53 us -> 6.13 us
    all_to_all x7, blocking collectives: 91.7 us -> 87 us  [exchange(): lax.all_to_all(x, axis, 0, 0, tiled=True, axis_index_groups=[ORDER[axis]])]
    all_to_all x1, waiting for transfers between devices: 4.6 us -> 0.01 us  [exchange(): lax.all_to_all(x, axis, 0, 0, tiled=True, axis_index_groups=[ORDER[axis]])]
    all_to_all x1, starting transfers between devices: 11.9 us -> 13.9 us  [exchange(): lax.all_to_all(x, axis, 0, 0, tiled=True, axis_index_groups=[ORDER[axis]])]
  transfers between devices with their start and end apart: 1 -> 1, of which waited for: 1 -> 0; matrix products, arithmetic and copies ran while one was open for 3% -> 4% of each run, Pallas kernels for 0% -> 0%
where the time goes in v3:
time: 113 us; the launch traced here: 112 us
  blocking collectives  87 us (77%)
  starting transfers between devices  13.9 us (12%)
  Pallas kernels  6.13 us (5%)
  local copies, waits for them, and re-layouts  4.39 us (4%)
    all_to_all x7, blocking collectives, exchange(): lax.all_to_all(x, axis, 0, 0, tiled=True, axis_index_groups=[ORDER[axis]])  87 us
    all_to_all x1, starting transfers between devices, exchange(): lax.all_to_all(x, axis, 0, 0, tiled=True, axis_index_groups=[ORDER[axis]])  13.9 us
    pallas_call x9, Pallas kernels, call(): pl.pallas_call(body, out_shape=out_shape, in_specs=[VMEM] * len(args) if...  6.13 us
    unnamed x19, local copies, waits for them, and re-layouts  4.39 us
  transfers between devices with their start and end apart: 1, of which 0 were waited for; matrix products, arithmetic and copies ran while one was open for 4% of the time, Pallas kernels for 0%

profile of v3, /device:TPU:1, one launch (start us, length us, event | category | flops | bytes accessed | tf_op | source)
XLA Modules:
  0.0 112.2 jit_solution(3210953580888585574)
XLA Ops:
  0.6 2.0 %shard_map.131 = f32[256,128]{1,0:T(8,128)} custom-call(bf16[2,8,256]{2,1,0:T(8,128)(2,1)} %tokens.1, bf16[256]{0:T(256)(128)(2,1)} %gain_at.1, bf16[256,1024]{1,0:T(8,128)(2,1)} %w_query_at.1, bf16[256,2,128]{2,1,0:T(2,128)(2,1)} %w_kv_at.1), custom_call_target="tpu_custom_call" | custom-call | tf_op jit(solution)/shard_map/pallas_call | solution.py:38
  2.7 13.9 %all-to-all-start = ((f32[32,8,128]{2,1,0:T(8,128)}), f32[32,8,128]{2,1,0:T(8,128)S(1)}, u32[]{:S(2)}, u32[]{:S(2)}) async-start(f32[32,8,128]{2,1,0:T(8,128)} %bitcast.11), calls=%async_computation | async-start | bytes 262144 | tf_op jit(solution)/shard_map/all_to_all | solution.py:34
  16.6 0.0 copy-start.1
  16.6 4.3 %copy.16 = bf16[256,2,3584]{2,0,1:T(8,128)(2,1)} copy(bf16[256,2,3584]{2,1,0:T(2,128)(2,1)} %param.18) | data formatting | bytes 7340032 | tf_op args[6]
  21.0 0.0 all-to-all-done.got
  21.0 0.0 copy-done.1
  21.0 0.0 copy-start.6
  21.0 0.0 copy-start.7
  21.0 11.4 %all_to_all.40.whole = bf16[32,8,128]{2,1,0:T(8,128)(2,1)S(1)} all-to-all(bf16[32,8,128]{2,1,0:T(8,128)(2,1)S(1)} %shard_map.132), channel_id=1, replica_groups={{144,152,128,136,176,184,160,168,208,216,192,200,240,248,224,232,16,24,..., dimensions={0} | all-to-all | bytes 131072 | tf_op jit(solution)/shard_map/all_to_all | solution.py:34
  32.5 0.0 copy-done.2
  32.5 0.0 copy-done.6
  32.5 0.0 copy-done.7
  32.5 0.0 copy-start.4
  32.5 0.0 copy-start
  32.5 0.0 copy-start.5
  32.5 0.0 copy-start.8
  32.5 1.5 %shard_map.133 = (f32[32,8,128]{2,1,0:T(8,128)S(1)}, bf16[1,2,8,1,2,128]{5,4,3,2,1,0:T(2,128)(2,1)}) custom-call(s32[8]{0:T(128)S(1)} %copy-done.6, s32[2]{0:T(128)S(1)} %copy-done.7, bf16[32,8,128]{2,1,0:T(8,128)(2,1)S(1)} %all_to_all.40.whole, bf16[8,1024,128]{2,1,0:T(8,128)(2,1)S(1)} %bitcast.10, bf16[8,1024,128]{2,1,0:T(8,128)(2,1)S(1)} %bitcast.9), custom_call_target="tpu_custom_call" | custom-call | tf_op jit(solution)/shard_map/pallas_call | solution.py:38
  34.0 12.6 %all_to_all.41.got = f32[32,8,128]{2,1,0:T(8,128)S(1)} all-to-all(f32[32,8,128]{2,1,0:T(8,128)S(1)} %get-tuple-element.6), channel_id=1, replica_groups={{144,152,128,136,176,184,160,168,208,216,192,200,240,248,224,232,16,24,..., dimensions={0} | all-to-all | bytes 262144 | tf_op jit(solution)/shard_map/all_to_all | solution.py:34
  46.6 0.2 shard_map.134
  46.8 11.4 %all_to_all.42.whole = bf16[32,4,128]{2,1,0:T(4,128)(2,1)S(1)} all-to-all(bf16[32,4,128]{2,1,0:T(4,128)(2,1)S(1)} %shard_map.134), channel_id=1, replica_groups={{144,152,128,136,176,184,160,168,208,216,192,200,240,248,224,232,16,24,..., dimensions={0} | all-to-all | bytes 65536 | tf_op jit(solution)/shard_map/all_to_all | solution.py:34
  58.1 0.0 copy-done.4
  58.1 0.2 shard_map.135
  58.3 12.7 %all_to_all.43.got = f32[8,16,256]{2,1,0:T(8,128)S(1)} all-to-all(f32[8,16,256]{2,1,0:T(8,128)S(1)} %shard_map.135), channel_id=1, replica_groups={{4,5,6,7,0,1,2,3},{12,13,14,15,8,9,10,11},{20,21,22,23,16,17,18,19},{28..., dimensions={0} | all-to-all | bytes 262144 | tf_op jit(solution)/shard_map/all_to_all | solution.py:34
  71.0 0.0 copy-done
  71.0 0.0 copy-start.3
  71.0 1.0 shard_map.136
  72.1 16.1 %all_to_all.44.got = s16[32,32,128]{2,1,0:T(8,128)(2,1)S(1)} all-to-all(s16[32,32,128]{2,1,0:T(8,128)(2,1)S(1)} %get-tuple-element.8), channel_id=1, replica_groups={{144,152,128,136,176,184,160,168,208,216,192,200,240,248,224,232,16,24,..., dimensions={0} | all-to-all | bytes 524288 | tf_op jit(solution)/shard_map/all_to_all | solution.py:34
  88.2 0.1 shard_map.137
  88.4 12.5 %all_to_all.45.whole = bf16[32,16,128]{2,1,0:T(8,128)(2,1)S(1)} all-to-all(bf16[32,16,128]{2,1,0:T(8,128)(2,1)S(1)} %shard_map.137), channel_id=1, replica_groups={{144,152,128,136,176,184,160,168,208,216,192,200,240,248,224,232,16,24,..., dimensions={0} | all-to-all | bytes 262144 | tf_op jit(solution)/shard_map/all_to_all | solution.py:34
  100.8 0.4 shard_map.138
  101.2 10.4 %all_to_all.46.got = f32[8,16,256]{2,1,0:T(8,128)S(1)} all-to-all(f32[8,16,256]{2,1,0:T(8,128)S(1)} %shard_map.138), channel_id=1, replica_groups={{4,5,6,7,0,1,2,3},{12,13,14,15,8,9,10,11},{20,21,22,23,16,17,18,19},{28..., dimensions={0} | all-to-all | bytes 262144 | tf_op jit(solution)/shard_map/all_to_all | solution.py:34
  111.6 0.6 shard_map.139
  (5 shorter events, 0.1 us)
Async XLA Ops:
  2.7 18.3 %all-to-all-start = ((f32[32,8,128]{2,1,0:T(8,128)}), f32[32,8,128]{2,1,0:T(8,128)S(1)}, u32[]{:S(2)}, u32[]{:S(2)}) async-start(f32[32,8,128]{2,1,0:T(8,128)} %bitcast.11), calls=%async_computation | async-start | bytes 262144 | tf_op jit(solution)/shard_map/all_to_all | solution.py:34
  16.6 4.4 %copy-start.1 = (bf16[8,1,1024,128]{3,2,1,0:T(8,128)(2,1)S(1)}, bf16[8,1,1024,128]{3,2,1,0:T(8,128)(2,1)}, u32[]{:S(2)}) copy-start(bf16[8,1,1024,128]{3,2,1,0:T(8,128)(2,1)} %param.21) | copy-start | bytes 6291460
  21.0 11.5 %copy-start.2 = (bf16[8,1,1024,128]{3,2,1,0:T(8,128)(2,1)S(1)}, bf16[8,1,1024,128]{3,2,1,0:T(8,128)(2,1)}, u32[]{:S(2)}) copy-start(bf16[8,1,1024,128]{3,2,1,0:T(8,128)(2,1)} %param.20) | copy-start | bytes 6291460
  21.0 11.5 %copy-start.6 = (s32[8]{0:T(128)S(1)}, s32[8]{0:T(128)}, u32[]{:S(2)}) copy-start(s32[8]{0:T(128)} %lengths.1) | copy-start | bytes 100
  21.0 11.5 %copy-start.7 = (s32[2]{0:T(128)S(1)}, s32[2]{0:T(128)}, u32[]{:S(2)}) copy-start(s32[2]{0:T(128)} %owner.1) | copy-start | bytes 28
  32.5 25.7 %copy-start.4 = (bf16[1024,256]{1,0:T(8,128)(2,1)S(1)}, bf16[1024,256]{1,0:T(8,128)(2,1)}, u32[]{:S(2)}) copy-start(bf16[1024,256]{1,0:T(8,128)(2,1)} %w.2) | copy-start | bytes 1572868
  32.5 38.5 %copy-start = (bf16[256,2,3584]{2,0,1:T(8,128)(2,1)S(1)}, bf16[256,2,3584]{2,0,1:T(8,128)(2,1)}, u32[]{:S(2)}) copy-start(bf16[256,2,3584]{2,0,1:T(8,128)(2,1)} %copy.16) | copy-start | bytes 11010052
  32.5 38.5 %copy-start.5 = (bf16[2,8,256]{2,1,0:T(8,128)(2,1)S(1)}, bf16[2,8,256]{2,1,0:T(8,128)(2,1)}, u32[]{:S(2)}) copy-start(bf16[2,8,256]{2,1,0:T(8,128)(2,1)} %tokens.1) | copy-start | bytes 24580
  32.5 38.5 %copy-start.8 = (bf16[256]{0:T(256)(128)(2,1)S(1)}, bf16[256]{0:T(256)(128)(2,1)}, u32[]{:S(2)}) copy-start(bf16[256]{0:T(256)(128)(2,1)} %gain.1) | copy-start | bytes 1540
  71.0 29.8 %copy-start.3 = (bf16[3584,256]{1,0:T(8,128)(2,1)S(1)}, bf16[3584,256]{1,0:T(8,128)(2,1)}, u32[]{:S(2)}) copy-start(bf16[3584,256]{1,0:T(8,128)(2,1)} %w.3) | copy-start | bytes 5505028

commit v4 on v3

--- a/solution.py
+++ b/solution.py
@@ -27,11 +27,12 @@
     ]
 
 
-ORDER = {"kv": ring((8, 4), (4, 2)), "head": ring((4, 2), (2, 0))}
-
-
-def exchange(x, axis):
-    return lax.all_to_all(x, axis, 0, 0, tiled=True, axis_index_groups=[ORDER[axis]])
+SCATTER, GATHER, HEAD = ring((8, 4), (5, 2)), ring((8, 4), (4, 2)), ring((4, 2), (2, 0))
+TURN = 4
+
+
+def exchange(x, axis, order):
+    return lax.all_to_all(x, axis, 0, 0, tiled=True, axis_index_groups=[order])
 
 
 def call(body, out_shape, args, specs=None, scratch=(), limit=24):
@@ -105,8 +106,9 @@
     for b in range(rollouts):
         tiles, pairs = [], []
         for s in range(2):
-            low = whole[(s * rollouts + b) * 2].astype(F32)
-            high = whole[(s * rollouts + b) * 2 + 1].astype(F32)
+            at = ((s * rollouts + b) * 2 + TURN) % whole.shape[0]
+            low = whole[at].astype(F32)
+            high = whole[at + 1].astype(F32)
             tiles.append(jnp.where(row < 4, low, pltpu.roll(high, 4, 0)))
             pairs.append((low[4:5], high[4:5]))
             pair = jnp.concatenate(pairs[s], 0)
@@ -172,6 +174,7 @@
         for slot in range(used)
     ]
     part = jnp.dot(jnp.concatenate(parts, 1), w[...], preferred_element_type=F32)
+    part = jnp.concatenate([part[TURN // 2 :], part[: TURN // 2]], 0)
     out[...] = jnp.broadcast_to(part[None], out.shape)
 
 
@@ -257,7 +260,7 @@
         + [pltpu.VMEM((2 * width, hd), F32), pltpu.SemaphoreType.DMA((4,))],
         60,
     )
-    got = exchange(chunk.reshape(kv_count, 8, hd), "kv")
+    got = exchange(chunk.reshape(kv_count, 8, hd), "kv", SCATTER)
     cache_shape = (rollouts, span, hd)
     keys, values = cache_keys.reshape(cache_shape), cache_values.reshape(cache_shape)
     mine = call(
@@ -267,7 +270,7 @@
         [VMEM, ANY, VMEM],
         limit=51,
     )
-    whole = exchange(mine, "kv")
+    whole = exchange(mine, "kv", GATHER)
 
     chunk, stored = call(
         attend,
@@ -275,15 +278,15 @@
         (lengths, owner, whole, keys, values),
         [VMEM] * 5,
     )
-    got = exchange(chunk, "kv")
-    context = exchange(call(combine, shape((kv_count, 4, hd), BF16), (got,)), "kv")
+    got = exchange(chunk, "kv", SCATTER)
+    context = exchange(call(combine, shape((kv_count, 4, hd), BF16), (got,)), "kv", GATHER)
     part = call(
         functools.partial(gathered_dot, 4),
         shape((head_count, rows, width), F32),
         (context, w_out),
         scratch=[pltpu.VMEM((kv_count * 4, hd), F32)],
     )
-    got = exchange(part, "head")
+    got = exchange(part, "head", HEAD)
 
     resid, chunk = call(
         gate_up,
@@ -291,15 +294,15 @@
         (got, tokens, norm_ffn, w_gate_up),
         scratch=[pltpu.VMEM((kv_count * 32, hd), F32)],
     )
-    got = exchange(chunk, "kv")
-    hidden = exchange(call(activate, shape((kv_count, 16, hd), BF16), (got,)), "kv")
+    got = exchange(chunk, "kv", SCATTER)
+    hidden = exchange(call(activate, shape((kv_count, 16, hd), BF16), (got,)), "kv", GATHER)
     part = call(
         functools.partial(gathered_dot, w_down.shape[0] // 2 // hd),
         shape((head_count, rows, width), F32),
         (hidden, w_down),
         scratch=[pltpu.VMEM((kv_count * 16, hd), F32)],
     )
-    got = exchange(part, "head")
+    got = exchange(part, "head", HEAD)
     layer_out = call(close, shape((steps, rollouts, width), BF16), (resid, got))
     return (layer_out, stored)
 

time: 113 us -> 113 us (level)
  transfers between devices with their start and end apart: 1 -> 1, of which waited for: 0 -> 1; matrix products, arithmetic and copies ran while one was open for 4% -> 4% of each run, Pallas kernels for 0% -> 0%
where the time goes in v4:
time: 113 us
  blocking collectives  87.9 us (78%)
  starting transfers between devices  13.3 us (12%)
  Pallas kernels  6.14 us (5%)
  local copies, waits for them, and re-layouts  4.39 us (4%)
    all_to_all x7, blocking collectives, exchange(): return lax.all_to_all(x, axis, 0, 0, tiled=True, axis_index_groups=[order])  87.9 us
    all_to_all x1, starting transfers between devices, exchange(): return lax.all_to_all(x, axis, 0, 0, tiled=True, axis_index_groups=[order])  13.3 us
    pallas_call x9, Pallas kernels, call(): pl.pallas_call(body, out_shape=out_shape, in_specs=[VMEM] * len(args) if...  6.14 us
    unnamed x19, local copies, waits for them, and re-layouts  4.39 us
  transfers between devices with their start and end apart: 1, of which 1 were waited for; matrix products, arithmetic and copies ran while one was open for 4% of the time, Pallas kernels for 0%

profile of v4, /device:TPU:1, one launch (start us, length us, event | category | flops | bytes accessed | tf_op | source)
XLA Modules:
  0.0 112.7 jit_solution(3297837432181250648)
XLA Ops:
  0.6 2.0 %shard_map.131 = f32[256,128]{1,0:T(8,128)} custom-call(bf16[2,8,256]{2,1,0:T(8,128)(2,1)} %tokens.1, bf16[256]{0:T(256)(128)(2,1)} %gain_at.1, bf16[256,1024]{1,0:T(8,128)(2,1)} %w_query_at.1, bf16[256,2,128]{2,1,0:T(2,128)(2,1)} %w_kv_at.1), custom_call_target="tpu_custom_call" | custom-call | tf_op jit(solution)/shard_map/pallas_call | solution.py:39
  2.7 13.3 %all-to-all-start = ((f32[32,8,128]{2,1,0:T(8,128)}), f32[32,8,128]{2,1,0:T(8,128)S(1)}, u32[]{:S(2)}, u32[]{:S(2)}) async-start(f32[32,8,128]{2,1,0:T(8,128)} %bitcast.11), calls=%async_computation | async-start | bytes 262144 | tf_op jit(solution)/shard_map/all_to_all | solution.py:35
  16.0 0.0 copy-start.1
  16.0 4.3 %copy.16 = bf16[256,2,3584]{2,0,1:T(8,128)(2,1)} copy(bf16[256,2,3584]{2,1,0:T(2,128)(2,1)} %param.18) | data formatting | bytes 7340032 | tf_op args[6]
  20.4 0.2 all-to-all-done.got
  20.6 0.0 copy-done.1
  20.6 11.4 %all_to_all.40.whole = bf16[32,8,128]{2,1,0:T(8,128)(2,1)S(1)} all-to-all(bf16[32,8,128]{2,1,0:T(8,128)(2,1)S(1)} %shard_map.132), channel_id=1, replica_groups={{144,152,128,136,176,184,160,168,208,216,192,200,240,248,224,232,16,24,..., dimensions={0} | all-to-all | bytes 131072 | tf_op jit(solution)/shard_map/all_to_all | solution.py:35
  32.0 0.0 copy-done.2
  32.1 0.0 copy-done.6
  32.1 0.0 copy-done.7
  32.1 0.0 copy-start.4
  32.1 0.0 copy-start
  32.1 0.0 copy-start.5
  32.1 0.0 copy-start.8
  32.1 1.5 %shard_map.133 = (f32[32,8,128]{2,1,0:T(8,128)S(1)}, bf16[1,2,8,1,2,128]{5,4,3,2,1,0:T(2,128)(2,1)}) custom-call(s32[8]{0:T(128)S(1)} %copy-done.6, s32[2]{0:T(128)S(1)} %copy-done.7, bf16[32,8,128]{2,1,0:T(8,128)(2,1)S(1)} %all_to_all.40.whole, bf16[8,1024,128]{2,1,0:T(8,128)(2,1)S(1)} %bitcast.10, bf16[8,1024,128]{2,1,0:T(8,128)(2,1)S(1)} %bitcast.9), custom_call_target="tpu_custom_call" | custom-call | tf_op jit(solution)/shard_map/pallas_call | solution.py:39
  33.6 13.5 %all_to_all.41.got = f32[32,8,128]{2,1,0:T(8,128)S(1)} all-to-all(f32[32,8,128]{2,1,0:T(8,128)S(1)} %get-tuple-element.6), channel_id=1, replica_groups={{176,184,160,168,208,216,192,200,240,248,224,232,16,24,0,8,48,56,32,40,..., dimensions={0} | all-to-all | bytes 262144 | tf_op jit(solution)/shard_map/all_to_all | solution.py:35
  47.1 0.2 shard_map.134
  47.3 10.8 %all_to_all.42.whole = bf16[32,4,128]{2,1,0:T(4,128)(2,1)S(1)} all-to-all(bf16[32,4,128]{2,1,0:T(4,128)(2,1)S(1)} %shard_map.134), channel_id=1, replica_groups={{144,152,128,136,176,184,160,168,208,216,192,200,240,248,224,232,16,24,..., dimensions={0} | all-to-all | bytes 65536 | tf_op jit(solution)/shard_map/all_to_all | solution.py:35
  58.1 0.0 copy-done.4
  58.1 0.2 shard_map.135
  58.3 13.3 %all_to_all.43.got = f32[8,16,256]{2,1,0:T(8,128)S(1)} all-to-all(f32[8,16,256]{2,1,0:T(8,128)S(1)} %shard_map.135), channel_id=1, replica_groups={{4,5,6,7,0,1,2,3},{12,13,14,15,8,9,10,11},{20,21,22,23,16,17,18,19},{28..., dimensions={0} | all-to-all | bytes 262144 | tf_op jit(solution)/shard_map/all_to_all | solution.py:35
  71.6 0.0 copy-done
  71.6 0.0 copy-done.5
  71.6 0.0 copy-done.8
  71.6 0.0 copy-start.3
  71.6 1.0 shard_map.136
  72.6 15.4 %all_to_all.44.got = s16[32,32,128]{2,1,0:T(8,128)(2,1)S(1)} all-to-all(s16[32,32,128]{2,1,0:T(8,128)(2,1)S(1)} %get-tuple-element.8), channel_id=1, replica_groups={{176,184,160,168,208,216,192,200,240,248,224,232,16,24,0,8,48,56,32,40,..., dimensions={0} | all-to-all | bytes 524288 | tf_op jit(solution)/shard_map/all_to_all | solution.py:35
  88.1 0.1 shard_map.137
  88.2 12.5 %all_to_all.45.whole = bf16[32,16,128]{2,1,0:T(8,128)(2,1)S(1)} all-to-all(bf16[32,16,128]{2,1,0:T(8,128)(2,1)S(1)} %shard_map.137), channel_id=1, replica_groups={{144,152,128,136,176,184,160,168,208,216,192,200,240,248,224,232,16,24,..., dimensions={0} | all-to-all | bytes 262144 | tf_op jit(solution)/shard_map/all_to_all | solution.py:35
  100.7 0.4 shard_map.138
  101.1 11.0 %all_to_all.46.got = f32[8,16,256]{2,1,0:T(8,128)S(1)} all-to-all(f32[8,16,256]{2,1,0:T(8,128)S(1)} %shard_map.138), channel_id=1, replica_groups={{4,5,6,7,0,1,2,3},{12,13,14,15,8,9,10,11},{20,21,22,23,16,17,18,19},{28..., dimensions={0} | all-to-all | bytes 262144 | tf_op jit(solution)/shard_map/all_to_all | solution.py:35
  112.1 0.6 shard_map.139
  (5 shorter events, 0.1 us)
Async XLA Ops:
  2.7 17.9 %all-to-all-start = ((f32[32,8,128]{2,1,0:T(8,128)}), f32[32,8,128]{2,1,0:T(8,128)S(1)}, u32[]{:S(2)}, u32[]{:S(2)}) async-start(f32[32,8,128]{2,1,0:T(8,128)} %bitcast.11), calls=%async_computation | async-start | bytes 262144 | tf_op jit(solution)/shard_map/all_to_all | solution.py:35
  16.0 4.6 %copy-start.1 = (bf16[8,1,1024,128]{3,2,1,0:T(8,128)(2,1)S(1)}, bf16[8,1,1024,128]{3,2,1,0:T(8,128)(2,1)}, u32[]{:S(2)}) copy-start(bf16[8,1,1024,128]{3,2,1,0:T(8,128)(2,1)} %param.21) | copy-start | bytes 6291460
  20.6 11.5 %copy-start.2 = (bf16[8,1,1024,128]{3,2,1,0:T(8,128)(2,1)S(1)}, bf16[8,1,1024,128]{3,2,1,0:T(8,128)(2,1)}, u32[]{:S(2)}) copy-start(bf16[8,1,1024,128]{3,2,1,0:T(8,128)(2,1)} %param.20) | copy-start | bytes 6291460
  20.6 11.5 %copy-start.6 = (s32[8]{0:T(128)S(1)}, s32[8]{0:T(128)}, u32[]{:S(2)}) copy-start(s32[8]{0:T(128)} %lengths.1) | copy-start | bytes 100
  20.6 11.5 %copy-start.7 = (s32[2]{0:T(128)S(1)}, s32[2]{0:T(128)}, u32[]{:S(2)}) copy-start(s32[2]{0:T(128)} %owner.1) | copy-start | bytes 28
  32.1 26.0 %copy-start.4 = (bf16[1024,256]{1,0:T(8,128)(2,1)S(1)}, bf16[1024,256]{1,0:T(8,128)(2,1)}, u32[]{:S(2)}) copy-start(bf16[1024,256]{1,0:T(8,128)(2,1)} %w.2) | copy-start | bytes 1572868
  32.1 39.5 %copy-start = (bf16[256,2,3584]{2,0,1:T(8,128)(2,1)S(1)}, bf16[256,2,3584]{2,0,1:T(8,128)(2,1)}, u32[]{:S(2)}) copy-start(bf16[256,2,3584]{2,0,1:T(8,128)(2,1)} %copy.16) | copy-start | bytes 11010052
  32.1 39.5 %copy-start.5 = (bf16[2,8,256]{2,1,0:T(8,128)(2,1)S(1)}, bf16[2,8,256]{2,1,0:T(8,128)(2,1)}, u32[]{:S(2)}) copy-start(bf16[2,8,256]{2,1,0:T(8,128)(2,1)} %tokens.1) | copy-start | bytes 24580
  32.1 39.5 %copy-start.8 = (bf16[256]{0:T(256)(128)(2,1)S(1)}, bf16[256]{0:T(256)(128)(2,1)}, u32[]{:S(2)}) copy-start(bf16[256]{0:T(256)(128)(2,1)} %gain.1) | copy-start | bytes 1540
  71.6 29.1 %copy-start.3 = (bf16[3584,256]{1,0:T(8,128)(2,1)S(1)}, bf16[3584,256]{1,0:T(8,128)(2,1)}, u32[]{:S(2)}) copy-start(bf16[3584,256]{1,0:T(8,128)(2,1)} %w.3) | copy-start | bytes 5505028

commit v5 on v4

--- a/solution.py
+++ b/solution.py
@@ -18,17 +18,21 @@
 ANY = pl.BlockSpec(memory_space=pl.ANY)
 
 
-def ring(sizes, first):
+def by_distance(sizes, first, steps):
     major, minor = sizes
-    return [
-        (a + first[0]) % major * minor + (b + first[1]) % minor
-        for a in range(major)
-        for b in range(minor)
-    ]
-
-
-SCATTER, GATHER, HEAD = ring((8, 4), (5, 2)), ring((8, 4), (4, 2)), ring((4, 2), (2, 0))
-TURN = 4
+
+    def distance(index):
+        at = (index // minor, index % minor)
+        hops = [min((p - q) % n, (q - p) % n) for p, q, n in zip(at, first, sizes)]
+        return hops[0] * steps[0] + hops[1] * steps[1]
+
+    return sorted(range(major * minor), key=distance)
+
+
+SCATTER = by_distance((8, 4), (5, 2), (2, 3))
+GATHER = by_distance((8, 4), (5, 2), (2, 3))
+HEAD = by_distance((4, 2), (2, 0), (2, 1))
+PLACE = [GATHER.index(device) for device in SCATTER]
 
 
 def exchange(x, axis, order):
@@ -106,9 +110,9 @@
     for b in range(rollouts):
         tiles, pairs = [], []
         for s in range(2):
-            at = ((s * rollouts + b) * 2 + TURN) % whole.shape[0]
-            low = whole[at].astype(F32)
-            high = whole[at + 1].astype(F32)
+            at = (s * rollouts + b) * 2
+            low = whole[PLACE[at]].astype(F32)
+            high = whole[PLACE[at + 1]].astype(F32)
             tiles.append(jnp.where(row < 4, low, pltpu.roll(high, 4, 0)))
             pairs.append((low[4:5], high[4:5]))
             pair = jnp.concatenate(pairs[s], 0)
@@ -166,7 +170,8 @@
 
 def gathered_dot(used, whole, w, out, wide):
     chunks, lines = whole.shape[:2]
-    wide[...] = whole[...].astype(F32).reshape(chunks * lines, LANES)
+    for c in range(chunks):
+        wide[c * lines : (c + 1) * lines] = whole[PLACE[c]].astype(F32)
     rows = chunks // 2
     parts = [
         wide[pl.ds(half * lines + slot, rows, stride=2 * lines), :].astype(BF16)
@@ -174,7 +179,6 @@
         for slot in range(used)
     ]
     part = jnp.dot(jnp.concatenate(parts, 1), w[...], preferred_element_type=F32)
-    part = jnp.concatenate([part[TURN // 2 :], part[: TURN // 2]], 0)
     out[...] = jnp.broadcast_to(part[None], out.shape)
 
 

time: 113 us -> 113 us (level)
  transfers between devices with their start and end apart: 1 -> 1, of which waited for: 1 -> 0; matrix products, arithmetic and copies ran while one was open for 4% -> 4% of each run, Pallas kernels for 0% -> 0%
where the time goes in v5:
time: 113 us
  blocking collectives  88 us (78%)
  starting transfers between devices  13.5 us (12%)
  Pallas kernels  6.13 us (5%)
  local copies, waits for them, and re-layouts  4.39 us (4%)
    all_to_all x7, blocking collectives, exchange(): return lax.all_to_all(x, axis, 0, 0, tiled=True, axis_index_groups=[order])  88 us
    all_to_all x1, starting transfers between devices, exchange(): return lax.all_to_all(x, axis, 0, 0, tiled=True, axis_index_groups=[order])  13.5 us
    pallas_call x9, Pallas kernels, call(): pl.pallas_call(body, out_shape=out_shape, in_specs=[VMEM] * len(args) if...  6.13 us
    unnamed x19, local copies, waits for them, and re-layouts  4.39 us
  transfers between devices with their start and end apart: 1, of which 0 were waited for; matrix products, arithmetic and copies ran while one was open for 4% of the time, Pallas kernels for 0%

profile of v5, /device:TPU:1, one launch (start us, length us, event | category | flops | bytes accessed | tf_op | source)
XLA Modules:
  0.0 112.8 jit_solution(10722512265650352927)
XLA Ops:
  0.6 2.0 %shard_map.131 = f32[256,128]{1,0:T(8,128)} custom-call(bf16[2,8,256]{2,1,0:T(8,128)(2,1)} %tokens.1, bf16[256]{0:T(256)(128)(2,1)} %gain_at.1, bf16[256,1024]{1,0:T(8,128)(2,1)} %w_query_at.1, bf16[256,2,128]{2,1,0:T(2,128)(2,1)} %w_kv_at.1), custom_call_target="tpu_custom_call" | custom-call | tf_op jit(solution)/shard_map/pallas_call | solution.py:43
  2.7 13.5 %all-to-all-start = ((f32[32,8,128]{2,1,0:T(8,128)}), f32[32,8,128]{2,1,0:T(8,128)S(1)}, u32[]{:S(2)}, u32[]{:S(2)}) async-start(f32[32,8,128]{2,1,0:T(8,128)} %bitcast.11), calls=%async_computation | async-start | bytes 262144 | tf_op jit(solution)/shard_map/all_to_all | solution.py:39
  16.1 0.0 copy-start.1
  16.1 4.3 %copy.16 = bf16[256,2,3584]{2,0,1:T(8,128)(2,1)} copy(bf16[256,2,3584]{2,1,0:T(2,128)(2,1)} %param.18) | data formatting | bytes 7340032 | tf_op args[6]
  20.5 0.0 all-to-all-done.got
  20.5 0.0 copy-done.1
  20.5 0.0 copy-start.6
  20.5 0.0 copy-start.7
  20.6 12.4 %all_to_all.40.whole = bf16[32,8,128]{2,1,0:T(8,128)(2,1)S(1)} all-to-all(bf16[32,8,128]{2,1,0:T(8,128)(2,1)S(1)} %shard_map.132), channel_id=1, replica_groups={{176,144,208,168,184,112,240,136,152,200,216,16,80,160,104,120,232,248,..., dimensions={0} | all-to-all | bytes 131072 | tf_op jit(solution)/shard_map/all_to_all | solution.py:39
  33.0 0.0 copy-done.2
  33.0 0.0 copy-done.6
  33.0 0.0 copy-done.7
  33.0 0.0 copy-start.4
  33.0 0.0 copy-start.5
  33.1 0.0 copy-start.8
  33.1 1.5 %shard_map.133 = (f32[32,8,128]{2,1,0:T(8,128)S(1)}, bf16[1,2,8,1,2,128]{5,4,3,2,1,0:T(2,128)(2,1)}) custom-call(s32[8]{0:T(128)S(1)} %copy-done.6, s32[2]{0:T(128)S(1)} %copy-done.7, bf16[32,8,128]{2,1,0:T(8,128)(2,1)S(1)} %all_to_all.40.whole, bf16[8,1024,128]{2,1,0:T(8,128)(2,1)S(1)} %bitcast.10, bf16[8,1024,128]{2,1,0:T(8,128)(2,1)S(1)} %bitcast.9), custom_call_target="tpu_custom_call" | custom-call | tf_op jit(solution)/shard_map/pallas_call | solution.py:43
  34.6 12.6 %all_to_all.41.got = f32[32,8,128]{2,1,0:T(8,128)S(1)} all-to-all(f32[32,8,128]{2,1,0:T(8,128)S(1)} %get-tuple-element.6), channel_id=1, replica_groups={{176,144,208,168,184,112,240,136,152,200,216,16,80,160,104,120,232,248,..., dimensions={0} | all-to-all | bytes 262144 | tf_op jit(solution)/shard_map/all_to_all | solution.py:39
  47.2 0.2 shard_map.134
  47.3 11.8 %all_to_all.42.whole = bf16[32,4,128]{2,1,0:T(4,128)(2,1)S(1)} all-to-all(bf16[32,4,128]{2,1,0:T(4,128)(2,1)S(1)} %shard_map.134), channel_id=1, replica_groups={{176,144,208,168,184,112,240,136,152,200,216,16,80,160,104,120,232,248,..., dimensions={0} | all-to-all | bytes 65536 | tf_op jit(solution)/shard_map/all_to_all | solution.py:39
  59.2 0.2 shard_map.135
  59.4 12.3 %all_to_all.43.got = f32[8,16,256]{2,1,0:T(8,128)S(1)} all-to-all(f32[8,16,256]{2,1,0:T(8,128)S(1)} %shard_map.135), channel_id=1, replica_groups={{4,5,2,6,3,7,0,1},{12,13,10,14,11,15,8,9},{20,21,18,22,19,23,16,17},{28..., dimensions={0} | all-to-all | bytes 262144 | tf_op jit(solution)/shard_map/all_to_all | solution.py:39
  71.7 0.0 copy-done
  71.7 0.0 copy-done.8
  71.7 0.0 copy-start.3
  71.7 1.0 shard_map.136
  72.8 15.9 %all_to_all.44.got = s16[32,32,128]{2,1,0:T(8,128)(2,1)S(1)} all-to-all(s16[32,32,128]{2,1,0:T(8,128)(2,1)S(1)} %get-tuple-element.8), channel_id=1, replica_groups={{176,144,208,168,184,112,240,136,152,200,216,16,80,160,104,120,232,248,..., dimensions={0} | all-to-all | bytes 524288 | tf_op jit(solution)/shard_map/all_to_all | solution.py:39
  88.6 0.1 shard_map.137
  88.8 13.1 %all_to_all.45.whole = bf16[32,16,128]{2,1,0:T(8,128)(2,1)S(1)} all-to-all(bf16[32,16,128]{2,1,0:T(8,128)(2,1)S(1)} %shard_map.137), channel_id=1, replica_groups={{176,144,208,168,184,112,240,136,152,200,216,16,80,160,104,120,232,248,..., dimensions={0} | all-to-all | bytes 262144 | tf_op jit(solution)/shard_map/all_to_all | solution.py:39
  101.8 0.0 copy-done.3
  101.8 0.4 shard_map.138
  102.2 9.9 %all_to_all.46.got = f32[8,16,256]{2,1,0:T(8,128)S(1)} all-to-all(f32[8,16,256]{2,1,0:T(8,128)S(1)} %shard_map.138), channel_id=1, replica_groups={{4,5,2,6,3,7,0,1},{12,13,10,14,11,15,8,9},{20,21,18,22,19,23,16,17},{28..., dimensions={0} | all-to-all | bytes 262144 | tf_op jit(solution)/shard_map/all_to_all | solution.py:39
  112.2 0.6 shard_map.139
  (5 shorter events, 0.1 us)
Async XLA Ops:
  2.7 17.8 %all-to-all-start = ((f32[32,8,128]{2,1,0:T(8,128)}), f32[32,8,128]{2,1,0:T(8,128)S(1)}, u32[]{:S(2)}, u32[]{:S(2)}) async-start(f32[32,8,128]{2,1,0:T(8,128)} %bitcast.11), calls=%async_computation | async-start | bytes 262144 | tf_op jit(solution)/shard_map/all_to_all | solution.py:39
  16.1 4.4 %copy-start.1 = (bf16[8,1,1024,128]{3,2,1,0:T(8,128)(2,1)S(1)}, bf16[8,1,1024,128]{3,2,1,0:T(8,128)(2,1)}, u32[]{:S(2)}) copy-start(bf16[8,1,1024,128]{3,2,1,0:T(8,128)(2,1)} %param.21) | copy-start | bytes 6291460
  20.5 12.5 %copy-start.2 = (bf16[8,1,1024,128]{3,2,1,0:T(8,128)(2,1)S(1)}, bf16[8,1,1024,128]{3,2,1,0:T(8,128)(2,1)}, u32[]{:S(2)}) copy-start(bf16[8,1,1024,128]{3,2,1,0:T(8,128)(2,1)} %param.20) | copy-start | bytes 6291460
  20.5 12.5 %copy-start.6 = (s32[8]{0:T(128)S(1)}, s32[8]{0:T(128)}, u32[]{:S(2)}) copy-start(s32[8]{0:T(128)} %lengths.1) | copy-start | bytes 100
  20.5 12.5 %copy-start.7 = (s32[2]{0:T(128)S(1)}, s32[2]{0:T(128)}, u32[]{:S(2)}) copy-start(s32[2]{0:T(128)} %owner.1) | copy-start | bytes 28
  33.0 26.1 %copy-start.4 = (bf16[1024,256]{1,0:T(8,128)(2,1)S(1)}, bf16[1024,256]{1,0:T(8,128)(2,1)}, u32[]{:S(2)}) copy-start(bf16[1024,256]{1,0:T(8,128)(2,1)} %w.2) | copy-start | bytes 1572868
  33.0 38.7 %copy-start = (bf16[256,2,3584]{2,0,1:T(8,128)(2,1)S(1)}, bf16[256,2,3584]{2,0,1:T(8,128)(2,1)}, u32[]{:S(2)}) copy-start(bf16[256,2,3584]{2,0,1:T(8,128)(2,1)} %copy.16) | copy-start | bytes 11010052
  33.0 38.7 %copy-start.5 = (bf16[2,8,256]{2,1,0:T(8,128)(2,1)S(1)}, bf16[2,8,256]{2,1,0:T(8,128)(2,1)}, u32[]{:S(2)}) copy-start(bf16[2,8,256]{2,1,0:T(8,128)(2,1)} %tokens.1) | copy-start | bytes 24580
  33.1 38.7 %copy-start.8 = (bf16[256]{0:T(256)(128)(2,1)S(1)}, bf16[256]{0:T(256)(128)(2,1)}, u32[]{:S(2)}) copy-start(bf16[256]{0:T(256)(128)(2,1)} %gain.1) | copy-start | bytes 1540
  71.7 30.1 %copy-start.3 = (bf16[3584,256]{1,0:T(8,128)(2,1)S(1)}, bf16[3584,256]{1,0:T(8,128)(2,1)}, u32[]{:S(2)}) copy-start(bf16[3584,256]{1,0:T(8,128)(2,1)} %w.3) | copy-start | bytes 5505028

commit v6 on v4

--- a/solution.py
+++ b/solution.py
@@ -27,8 +27,9 @@
     ]
 
 
-SCATTER, GATHER, HEAD = ring((8, 4), (5, 2)), ring((8, 4), (4, 2)), ring((4, 2), (2, 0))
-TURN = 4
+FIRST, KV = ring((8, 4), (5, 2)), ring((8, 4), (4, 2))
+HEAD = [4, 5, 2, 6, 3, 7, 0, 1]
+PLACE = [KV.index(device) for device in FIRST]
 
 
 def exchange(x, axis, order):
@@ -106,9 +107,9 @@
     for b in range(rollouts):
         tiles, pairs = [], []
         for s in range(2):
-            at = ((s * rollouts + b) * 2 + TURN) % whole.shape[0]
-            low = whole[at].astype(F32)
-            high = whole[at + 1].astype(F32)
+            at = (s * rollouts + b) * 2
+            low = whole[PLACE[at]].astype(F32)
+            high = whole[PLACE[at + 1]].astype(F32)
             tiles.append(jnp.where(row < 4, low, pltpu.roll(high, 4, 0)))
             pairs.append((low[4:5], high[4:5]))
             pair = jnp.concatenate(pairs[s], 0)
@@ -174,7 +175,6 @@
         for slot in range(used)
     ]
     part = jnp.dot(jnp.concatenate(parts, 1), w[...], preferred_element_type=F32)
-    part = jnp.concatenate([part[TURN // 2 :], part[: TURN // 2]], 0)
     out[...] = jnp.broadcast_to(part[None], out.shape)
 
 
@@ -260,7 +260,7 @@
         + [pltpu.VMEM((2 * width, hd), F32), pltpu.SemaphoreType.DMA((4,))],
         60,
     )
-    got = exchange(chunk.reshape(kv_count, 8, hd), "kv", SCATTER)
+    got = exchange(chunk.reshape(kv_count, 8, hd), "kv", FIRST)
     cache_shape = (rollouts, span, hd)
     keys, values = cache_keys.reshape(cache_shape), cache_values.reshape(cache_shape)
     mine = call(
@@ -270,7 +270,7 @@
         [VMEM, ANY, VMEM],
         limit=51,
     )
-    whole = exchange(mine, "kv", GATHER)
+    whole = exchange(mine, "kv", KV)
 
     chunk, stored = call(
         attend,
@@ -278,8 +278,8 @@
         (lengths, owner, whole, keys, values),
         [VMEM] * 5,
     )
-    got = exchange(chunk, "kv", SCATTER)
-    context = exchange(call(combine, shape((kv_count, 4, hd), BF16), (got,)), "kv", GATHER)
+    got = exchange(chunk, "kv", KV)
+    context = exchange(call(combine, shape((kv_count, 4, hd), BF16), (got,)), "kv", KV)
     part = call(
         functools.partial(gathered_dot, 4),
         shape((head_count, rows, width), F32),
@@ -294,8 +294,8 @@
         (got, tokens, norm_ffn, w_gate_up),
         scratch=[pltpu.VMEM((kv_count * 32, hd), F32)],
     )
-    got = exchange(chunk, "kv", SCATTER)
-    hidden = exchange(call(activate, shape((kv_count, 16, hd), BF16), (got,)), "kv", GATHER)
+    got = exchange(chunk, "kv", KV)
+    hidden = exchange(call(activate, shape((kv_count, 16, hd), BF16), (got,)), "kv", KV)
     part = call(
         functools.partial(gathered_dot, w_down.shape[0] // 2 // hd),
         shape((head_count, rows, width), F32),

time: 113 us -> 113 us (level)
  no operation moved by 1% of the time
where the time goes in v6:
time: 113 us; the launch traced here: 112 us
  blocking collectives  87.3 us (77%)
  starting transfers between devices  13.3 us (12%)
  Pallas kernels  6.13 us (5%)
  local copies, waits for them, and re-layouts  4.39 us (4%)
    all_to_all x7, blocking collectives, exchange(): return lax.all_to_all(x, axis, 0, 0, tiled=True, axis_index_groups=[order])  87.3 us
    all_to_all x1, starting transfers between devices, exchange(): return lax.all_to_all(x, axis, 0, 0, tiled=True, axis_index_groups=[order])  13.3 us
    pallas_call x9, Pallas kernels, call(): pl.pallas_call(body, out_shape=out_shape, in_specs=[VMEM] * len(args) if...  6.13 us
    unnamed x19, local copies, waits for them, and re-layouts  4.39 us
  transfers between devices with their start and end apart: 1, of which 1 were waited for; matrix products, arithmetic and copies ran while one was open for 4% of the time, Pallas kernels for 0%

profile of v6, /device:TPU:1, one launch (start us, length us, event | category | flops | bytes accessed | tf_op | source)
XLA Modules:
  0.0 112.2 jit_solution(10758127223776179603)
XLA Ops:
  0.6 2.0 %shard_map.131 = f32[256,128]{1,0:T(8,128)} custom-call(bf16[2,8,256]{2,1,0:T(8,128)(2,1)} %tokens.1, bf16[256]{0:T(256)(128)(2,1)} %gain_at.1, bf16[256,1024]{1,0:T(8,128)(2,1)} %w_query_at.1, bf16[256,2,128]{2,1,0:T(2,128)(2,1)} %w_kv_at.1), custom_call_target="tpu_custom_call" | custom-call | tf_op jit(solution)/shard_map/pallas_call | solution.py:40
  2.7 13.3 %all-to-all-start = ((f32[32,8,128]{2,1,0:T(8,128)}), f32[32,8,128]{2,1,0:T(8,128)S(1)}, u32[]{:S(2)}, u32[]{:S(2)}) async-start(f32[32,8,128]{2,1,0:T(8,128)} %bitcast.11), calls=%async_computation | async-start | bytes 262144 | tf_op jit(solution)/shard_map/all_to_all | solution.py:36
  16.0 0.0 copy-start.1
  16.0 4.3 %copy.16 = bf16[256,2,3584]{2,0,1:T(8,128)(2,1)} copy(bf16[256,2,3584]{2,1,0:T(2,128)(2,1)} %param.18) | data formatting | bytes 7340032 | tf_op args[6]
  20.4 0.2 all-to-all-done.got
  20.6 0.0 copy-done.1
  20.6 11.4 %all_to_all.40.whole = bf16[32,8,128]{2,1,0:T(8,128)(2,1)S(1)} all-to-all(bf16[32,8,128]{2,1,0:T(8,128)(2,1)S(1)} %shard_map.132), channel_id=1, replica_groups={{144,152,128,136,176,184,160,168,208,216,192,200,240,248,224,232,16,24,..., dimensions={0} | all-to-all | bytes 131072 | tf_op jit(solution)/shard_map/all_to_all | solution.py:36
  32.0 0.0 copy-done.2
  32.1 0.0 copy-done.6
  32.1 0.0 copy-done.7
  32.1 0.0 copy-start.4
  32.1 0.0 copy-start
  32.1 0.0 copy-start.5
  32.1 0.0 copy-start.8
  32.1 1.5 %shard_map.133 = (f32[32,8,128]{2,1,0:T(8,128)S(1)}, bf16[1,2,8,1,2,128]{5,4,3,2,1,0:T(2,128)(2,1)}) custom-call(s32[8]{0:T(128)S(1)} %copy-done.6, s32[2]{0:T(128)S(1)} %copy-done.7, bf16[32,8,128]{2,1,0:T(8,128)(2,1)S(1)} %all_to_all.40.whole, bf16[8,1024,128]{2,1,0:T(8,128)(2,1)S(1)} %bitcast.10, bf16[8,1024,128]{2,1,0:T(8,128)(2,1)S(1)} %bitcast.9), custom_call_target="tpu_custom_call" | custom-call | tf_op jit(solution)/shard_map/pallas_call | solution.py:40
  33.6 12.3 %all_to_all.41.got = f32[32,8,128]{2,1,0:T(8,128)S(1)} all-to-all(f32[32,8,128]{2,1,0:T(8,128)S(1)} %get-tuple-element.6), channel_id=1, replica_groups={{144,152,128,136,176,184,160,168,208,216,192,200,240,248,224,232,16,24,..., dimensions={0} | all-to-all | bytes 262144 | tf_op jit(solution)/shard_map/all_to_all | solution.py:36
  45.9 0.2 shard_map.134
  46.1 11.7 %all_to_all.42.whole = bf16[32,4,128]{2,1,0:T(4,128)(2,1)S(1)} all-to-all(bf16[32,4,128]{2,1,0:T(4,128)(2,1)S(1)} %shard_map.134), channel_id=1, replica_groups={{144,152,128,136,176,184,160,168,208,216,192,200,240,248,224,232,16,24,..., dimensions={0} | all-to-all | bytes 65536 | tf_op jit(solution)/shard_map/all_to_all | solution.py:36
  57.7 0.0 copy-done.4
  57.7 0.2 shard_map.135
  57.9 13.1 %all_to_all.43.got = f32[8,16,256]{2,1,0:T(8,128)S(1)} all-to-all(f32[8,16,256]{2,1,0:T(8,128)S(1)} %shard_map.135), channel_id=1, replica_groups={{4,5,2,6,3,7,0,1},{12,13,10,14,11,15,8,9},{20,21,18,22,19,23,16,17},{28..., dimensions={0} | all-to-all | bytes 262144 | tf_op jit(solution)/shard_map/all_to_all | solution.py:36
  71.1 0.0 copy-done
  71.1 0.0 copy-done.5
  71.1 0.0 copy-start.3
  71.1 1.0 shard_map.136
  72.1 16.5 %all_to_all.44.got = s16[32,32,128]{2,1,0:T(8,128)(2,1)S(1)} all-to-all(s16[32,32,128]{2,1,0:T(8,128)(2,1)S(1)} %get-tuple-element.8), channel_id=1, replica_groups={{144,152,128,136,176,184,160,168,208,216,192,200,240,248,224,232,16,24,..., dimensions={0} | all-to-all | bytes 524288 | tf_op jit(solution)/shard_map/all_to_all | solution.py:36
  88.7 0.1 shard_map.137
  88.8 12.5 %all_to_all.45.whole = bf16[32,16,128]{2,1,0:T(8,128)(2,1)S(1)} all-to-all(bf16[32,16,128]{2,1,0:T(8,128)(2,1)S(1)} %shard_map.137), channel_id=1, replica_groups={{144,152,128,136,176,184,160,168,208,216,192,200,240,248,224,232,16,24,..., dimensions={0} | all-to-all | bytes 262144 | tf_op jit(solution)/shard_map/all_to_all | solution.py:36
  101.3 0.0 copy-done.3
  101.3 0.4 shard_map.138
  101.7 9.8 %all_to_all.46.got = f32[8,16,256]{2,1,0:T(8,128)S(1)} all-to-all(f32[8,16,256]{2,1,0:T(8,128)S(1)} %shard_map.138), channel_id=1, replica_groups={{4,5,2,6,3,7,0,1},{12,13,10,14,11,15,8,9},{20,21,18,22,19,23,16,17},{28..., dimensions={0} | all-to-all | bytes 262144 | tf_op jit(solution)/shard_map/all_to_all | solution.py:36
  111.5 0.6 shard_map.139
  (5 shorter events, 0.1 us)
Async XLA Ops:
  2.7 17.9 %all-to-all-start = ((f32[32,8,128]{2,1,0:T(8,128)}), f32[32,8,128]{2,1,0:T(8,128)S(1)}, u32[]{:S(2)}, u32[]{:S(2)}) async-start(f32[32,8,128]{2,1,0:T(8,128)} %bitcast.11), calls=%async_computation | async-start | bytes 262144 | tf_op jit(solution)/shard_map/all_to_all | solution.py:36
  16.0 4.6 %copy-start.1 = (bf16[8,1,1024,128]{3,2,1,0:T(8,128)(2,1)S(1)}, bf16[8,1,1024,128]{3,2,1,0:T(8,128)(2,1)}, u32[]{:S(2)}) copy-start(bf16[8,1,1024,128]{3,2,1,0:T(8,128)(2,1)} %param.21) | copy-start | bytes 6291460
  20.6 11.5 %copy-start.2 = (bf16[8,1,1024,128]{3,2,1,0:T(8,128)(2,1)S(1)}, bf16[8,1,1024,128]{3,2,1,0:T(8,128)(2,1)}, u32[]{:S(2)}) copy-start(bf16[8,1,1024,128]{3,2,1,0:T(8,128)(2,1)} %param.20) | copy-start | bytes 6291460
  20.6 11.5 %copy-start.6 = (s32[8]{0:T(128)S(1)}, s32[8]{0:T(128)}, u32[]{:S(2)}) copy-start(s32[8]{0:T(128)} %lengths.1) | copy-start | bytes 100
  20.6 11.5 %copy-start.7 = (s32[2]{0:T(128)S(1)}, s32[2]{0:T(128)}, u32[]{:S(2)}) copy-start(s32[2]{0:T(128)} %owner.1) | copy-start | bytes 28
  32.1 25.7 %copy-start.4 = (bf16[1024,256]{1,0:T(8,128)(2,1)S(1)}, bf16[1024,256]{1,0:T(8,128)(2,1)}, u32[]{:S(2)}) copy-start(bf16[1024,256]{1,0:T(8,128)(2,1)} %w.2) | copy-start | bytes 1572868
  32.1 39.0 %copy-start = (bf16[256,2,3584]{2,0,1:T(8,128)(2,1)S(1)}, bf16[256,2,3584]{2,0,1:T(8,128)(2,1)}, u32[]{:S(2)}) copy-start(bf16[256,2,3584]{2,0,1:T(8,128)(2,1)} %copy.16) | copy-start | bytes 11010052
  32.1 39.0 %copy-start.5 = (bf16[2,8,256]{2,1,0:T(8,128)(2,1)S(1)}, bf16[2,8,256]{2,1,0:T(8,128)(2,1)}, u32[]{:S(2)}) copy-start(bf16[2,8,256]{2,1,0:T(8,128)(2,1)} %tokens.1) | copy-start | bytes 24580
  32.1 39.0 %copy-start.8 = (bf16[256]{0:T(256)(128)(2,1)S(1)}, bf16[256]{0:T(256)(128)(2,1)}, u32[]{:S(2)}) copy-start(bf16[256]{0:T(256)(128)(2,1)} %gain.1) | copy-start | bytes 1540
  71.1 30.3 %copy-start.3 = (bf16[3584,256]{1,0:T(8,128)(2,1)S(1)}, bf16[3584,256]{1,0:T(8,128)(2,1)}, u32[]{:S(2)}) copy-start(bf16[3584,256]{1,0:T(8,128)(2,1)} %w.3) | copy-start | bytes 5505028

commit v7 on v6

--- a/solution.py
+++ b/solution.py
@@ -28,7 +28,7 @@
 
 
 FIRST, KV = ring((8, 4), (5, 2)), ring((8, 4), (4, 2))
-HEAD = [4, 5, 2, 6, 3, 7, 0, 1]
+HEAD, LAST = ring((4, 2), (2, 0)), [4, 5, 2, 6, 3, 7, 0, 1]
 PLACE = [KV.index(device) for device in FIRST]
 
 
@@ -118,16 +118,25 @@
         queries.append(jnp.concatenate(tiles, 0))
         news.append(pairs)
     scores = []
-    for b in range(rollouts):
-        scores.append(
+    for b in range(0, rollouts, 2):
+        blank = jnp.zeros_like(queries[b])
+        pair = jnp.concatenate(
+            [
+                jnp.concatenate([queries[b], blank], 1),
+                jnp.concatenate([blank, queries[b + 1]], 1),
+            ],
+            0,
+        )
+        both = (
             lax.dot_general(
-                queries[b].astype(BF16),
-                keys[b],
+                pair.astype(BF16),
+                jnp.concatenate([keys[b], keys[b + 1]], 1),
                 (((1,), (1,)), ((), ())),
                 preferred_element_type=F32,
             )
             * scale
         )
+        scores += [both[:16], both[16:]]
     weights, totals, tops, extras = [], [], [], []
     for b in range(rollouts):
         keep = column < live[:, b : b + 1]
@@ -145,8 +154,16 @@
         weights.append(e.astype(BF16))
         tops.append(top)
         extras.append(extra)
+    weighted = []
+    for b in range(0, rollouts, 2):
+        both = jnp.dot(
+            jnp.concatenate([weights[b], weights[b + 1]], 0),
+            jnp.concatenate([values[b], values[b + 1]], 1),
+            preferred_element_type=F32,
+        )
+        weighted += [both[:16, :hd], both[16:, hd:]]
     for b in range(rollouts):
-        sums = jnp.dot(weights[b], values[b], preferred_element_type=F32)
+        sums = weighted[b]
         for t in range(2):
             sums = sums + extras[b][t].astype(BF16).astype(F32) * news[b][t][1]
         stat = jnp.where(lane < LANES // 2, tops[b], totals[b])
@@ -302,7 +319,7 @@
         (hidden, w_down),
         scratch=[pltpu.VMEM((kv_count * 16, hd), F32)],
     )
-    got = exchange(part, "head", HEAD)
+    got = exchange(part, "head", LAST)
     layer_out = call(close, shape((steps, rollouts, width), BF16), (resid, got))
     return (layer_out, stored)
 

time: 113 us -> 113 us (level)
  no operation moved by 1% of the time
where the time goes in v7:
time: 113 us; the launch traced here: 112 us
  blocking collectives  87.5 us (77%)
  starting transfers between devices  13.3 us (12%)
  Pallas kernels  6.27 us (6%)
  local copies, waits for them, and re-layouts  4.39 us (4%)
    all_to_all x7, blocking collectives, exchange(): return lax.all_to_all(x, axis, 0, 0, tiled=True, axis_index_groups=[order])  87.5 us
    all_to_all x1, starting transfers between devices, exchange(): return lax.all_to_all(x, axis, 0, 0, tiled=True, axis_index_groups=[order])  13.3 us
    pallas_call x9, Pallas kernels, call(): pl.pallas_call(body, out_shape=out_shape, in_specs=[VMEM] * len(args) if...  6.27 us
    unnamed x19, local copies, waits for them, and re-layouts  4.39 us
  transfers between devices with their start and end apart: 1, of which 1 were waited for; matrix products, arithmetic and copies ran while one was open for 4% of the time, Pallas kernels for 0%

profile of v7, /device:TPU:1, one launch (start us, length us, event | category | flops | bytes accessed | tf_op | source)
XLA Modules:
  0.0 112.4 jit_solution(5349173967581700283)
XLA Ops:
  0.6 2.0 %shard_map.131 = f32[256,128]{1,0:T(8,128)} custom-call(bf16[2,8,256]{2,1,0:T(8,128)(2,1)} %tokens.1, bf16[256]{0:T(256)(128)(2,1)} %gain_at.1, bf16[256,1024]{1,0:T(8,128)(2,1)} %w_query_at.1, bf16[256,2,128]{2,1,0:T(2,128)(2,1)} %w_kv_at.1), custom_call_target="tpu_custom_call" | custom-call | tf_op jit(solution)/shard_map/pallas_call | solution.py:40
  2.7 13.3 %all-to-all-start = ((f32[32,8,128]{2,1,0:T(8,128)}), f32[32,8,128]{2,1,0:T(8,128)S(1)}, u32[]{:S(2)}, u32[]{:S(2)}) async-start(f32[32,8,128]{2,1,0:T(8,128)} %bitcast.11), calls=%async_computation | async-start | bytes 262144 | tf_op jit(solution)/shard_map/all_to_all | solution.py:36
  16.0 0.0 copy-start.1
  16.0 4.3 %copy.16 = bf16[256,2,3584]{2,0,1:T(8,128)(2,1)} copy(bf16[256,2,3584]{2,1,0:T(2,128)(2,1)} %param.18) | data formatting | bytes 7340032 | tf_op args[6]
  20.4 0.2 all-to-all-done.got
  20.6 0.0 copy-done.1
  20.6 11.4 %all_to_all.40.whole = bf16[32,8,128]{2,1,0:T(8,128)(2,1)S(1)} all-to-all(bf16[32,8,128]{2,1,0:T(8,128)(2,1)S(1)} %shard_map.132), channel_id=1, replica_groups={{144,152,128,136,176,184,160,168,208,216,192,200,240,248,224,232,16,24,..., dimensions={0} | all-to-all | bytes 131072 | tf_op jit(solution)/shard_map/all_to_all | solution.py:36
  32.0 0.0 copy-done.2
  32.1 0.0 copy-done.6
  32.1 0.0 copy-done.7
  32.1 0.0 copy-start.4
  32.1 0.0 copy-start
  32.1 0.0 copy-start.5
  32.1 0.0 copy-start.8
  32.1 1.6 %shard_map.133 = (f32[32,8,128]{2,1,0:T(8,128)S(1)}, bf16[1,2,8,1,2,128]{5,4,3,2,1,0:T(2,128)(2,1)}) custom-call(s32[8]{0:T(128)S(1)} %copy-done.6, s32[2]{0:T(128)S(1)} %copy-done.7, bf16[32,8,128]{2,1,0:T(8,128)(2,1)S(1)} %all_to_all.40.whole, bf16[8,1024,128]{2,1,0:T(8,128)(2,1)S(1)} %bitcast.10, bf16[8,1024,128]{2,1,0:T(8,128)(2,1)S(1)} %bitcast.9), custom_call_target="tpu_custom_call" | custom-call | tf_op jit(solution)/shard_map/pallas_call | solution.py:40
  33.8 12.3 %all_to_all.41.got = f32[32,8,128]{2,1,0:T(8,128)S(1)} all-to-all(f32[32,8,128]{2,1,0:T(8,128)S(1)} %get-tuple-element.6), channel_id=1, replica_groups={{144,152,128,136,176,184,160,168,208,216,192,200,240,248,224,232,16,24,..., dimensions={0} | all-to-all | bytes 262144 | tf_op jit(solution)/shard_map/all_to_all | solution.py:36
  46.0 0.2 shard_map.134
  46.2 11.7 %all_to_all.42.whole = bf16[32,4,128]{2,1,0:T(4,128)(2,1)S(1)} all-to-all(bf16[32,4,128]{2,1,0:T(4,128)(2,1)S(1)} %shard_map.134), channel_id=1, replica_groups={{144,152,128,136,176,184,160,168,208,216,192,200,240,248,224,232,16,24,..., dimensions={0} | all-to-all | bytes 65536 | tf_op jit(solution)/shard_map/all_to_all | solution.py:36
  57.9 0.0 copy-done.4
  57.9 0.2 shard_map.135
  58.1 12.9 %all_to_all.43.got = f32[8,16,256]{2,1,0:T(8,128)S(1)} all-to-all(f32[8,16,256]{2,1,0:T(8,128)S(1)} %shard_map.135), channel_id=1, replica_groups={{4,5,6,7,0,1,2,3},{12,13,14,15,8,9,10,11},{20,21,22,23,16,17,18,19},{28..., dimensions={0} | all-to-all | bytes 262144 | tf_op jit(solution)/shard_map/all_to_all | solution.py:36
  71.0 0.0 copy-done
  71.0 0.0 copy-done.5
  71.0 0.0 copy-done.8
  71.0 0.0 copy-start.3
  71.0 1.0 shard_map.136
  72.0 16.1 %all_to_all.44.got = s16[32,32,128]{2,1,0:T(8,128)(2,1)S(1)} all-to-all(s16[32,32,128]{2,1,0:T(8,128)(2,1)S(1)} %get-tuple-element.8), channel_id=1, replica_groups={{144,152,128,136,176,184,160,168,208,216,192,200,240,248,224,232,16,24,..., dimensions={0} | all-to-all | bytes 524288 | tf_op jit(solution)/shard_map/all_to_all | solution.py:36
  88.2 0.1 shard_map.137
  88.3 12.5 %all_to_all.45.whole = bf16[32,16,128]{2,1,0:T(8,128)(2,1)S(1)} all-to-all(bf16[32,16,128]{2,1,0:T(8,128)(2,1)S(1)} %shard_map.137), channel_id=1, replica_groups={{144,152,128,136,176,184,160,168,208,216,192,200,240,248,224,232,16,24,..., dimensions={0} | all-to-all | bytes 262144 | tf_op jit(solution)/shard_map/all_to_all | solution.py:36
  100.8 0.4 shard_map.138
  101.2 10.6 %all_to_all.46.got = f32[8,16,256]{2,1,0:T(8,128)S(1)} all-to-all(f32[8,16,256]{2,1,0:T(8,128)S(1)} %shard_map.138), channel_id=1, replica_groups={{4,5,2,6,3,7,0,1},{12,13,10,14,11,15,8,9},{20,21,18,22,19,23,16,17},{28..., dimensions={0} | all-to-all | bytes 262144 | tf_op jit(solution)/shard_map/all_to_all | solution.py:36
  111.8 0.6 shard_map.139
  (5 shorter events, 0.1 us)
Async XLA Ops:
  2.7 17.9 %all-to-all-start = ((f32[32,8,128]{2,1,0:T(8,128)}), f32[32,8,128]{2,1,0:T(8,128)S(1)}, u32[]{:S(2)}, u32[]{:S(2)}) async-start(f32[32,8,128]{2,1,0:T(8,128)} %bitcast.11), calls=%async_computation | async-start | bytes 262144 | tf_op jit(solution)/shard_map/all_to_all | solution.py:36
  16.0 4.6 %copy-start.1 = (bf16[8,1,1024,128]{3,2,1,0:T(8,128)(2,1)S(1)}, bf16[8,1,1024,128]{3,2,1,0:T(8,128)(2,1)}, u32[]{:S(2)}) copy-start(bf16[8,1,1024,128]{3,2,1,0:T(8,128)(2,1)} %param.21) | copy-start | bytes 6291460
  20.6 11.5 %copy-start.2 = (bf16[8,1,1024,128]{3,2,1,0:T(8,128)(2,1)S(1)}, bf16[8,1,1024,128]{3,2,1,0:T(8,128)(2,1)}, u32[]{:S(2)}) copy-start(bf16[8,1,1024,128]{3,2,1,0:T(8,128)(2,1)} %param.20) | copy-start | bytes 6291460
  20.6 11.5 %copy-start.6 = (s32[8]{0:T(128)S(1)}, s32[8]{0:T(128)}, u32[]{:S(2)}) copy-start(s32[8]{0:T(128)} %lengths.1) | copy-start | bytes 100
  20.6 11.5 %copy-start.7 = (s32[2]{0:T(128)S(1)}, s32[2]{0:T(128)}, u32[]{:S(2)}) copy-start(s32[2]{0:T(128)} %owner.1) | copy-start | bytes 28
  32.1 25.8 %copy-start.4 = (bf16[1024,256]{1,0:T(8,128)(2,1)S(1)}, bf16[1024,256]{1,0:T(8,128)(2,1)}, u32[]{:S(2)}) copy-start(bf16[1024,256]{1,0:T(8,128)(2,1)} %w.2) | copy-start | bytes 1572868
  32.1 38.9 %copy-start = (bf16[256,2,3584]{2,0,1:T(8,128)(2,1)S(1)}, bf16[256,2,3584]{2,0,1:T(8,128)(2,1)}, u32[]{:S(2)}) copy-start(bf16[256,2,3584]{2,0,1:T(8,128)(2,1)} %copy.16) | copy-start | bytes 11010052
  32.1 38.9 %copy-start.5 = (bf16[2,8,256]{2,1,0:T(8,128)(2,1)S(1)}, bf16[2,8,256]{2,1,0:T(8,128)(2,1)}, u32[]{:S(2)}) copy-start(bf16[2,8,256]{2,1,0:T(8,128)(2,1)} %tokens.1) | copy-start | bytes 24580
  32.1 38.9 %copy-start.8 = (bf16[256]{0:T(256)(128)(2,1)S(1)}, bf16[256]{0:T(256)(128)(2,1)}, u32[]{:S(2)}) copy-start(bf16[256]{0:T(256)(128)(2,1)} %gain.1) | copy-start | bytes 1540
  71.0 29.8 %copy-start.3 = (bf16[3584,256]{1,0:T(8,128)(2,1)S(1)}, bf16[3584,256]{1,0:T(8,128)(2,1)}, u32[]{:S(2)}) copy-start(bf16[3584,256]{1,0:T(8,128)(2,1)} %w.3) | copy-start | bytes 5505028

commit v8 on v6

--- a/solution.py
+++ b/solution.py
@@ -13,7 +13,7 @@
 F32 = jnp.float32
 BF16 = jnp.bfloat16
 LANES = 128
-TOP = 32767.0
+TOP = 32700.0
 VMEM = pl.BlockSpec(memory_space=pltpu.VMEM)
 ANY = pl.BlockSpec(memory_space=pl.ANY)
 
@@ -28,7 +28,7 @@
 
 
 FIRST, KV = ring((8, 4), (5, 2)), ring((8, 4), (4, 2))
-HEAD = [4, 5, 2, 6, 3, 7, 0, 1]
+HEAD, LAST = ring((4, 2), (2, 0)), [4, 5, 2, 6, 3, 7, 0, 1]
 PLACE = [KV.index(device) for device in FIRST]
 
 
@@ -50,11 +50,12 @@
 def project(
     tokens_at, gain_at, w_query_at, w_kv_at, out, tokens, gain, w_query, w_kv, wide, sems
 ):
+    across = w_query.shape[1] // 2
+    sides = [pl.ds(half * across, across) for half in range(2)]
+    pairs = [(w_kv_at, w_kv), (tokens_at, tokens), (gain_at, gain)]
+    pairs += [(w_query_at.at[:, side], w_query.at[:, side]) for side in sides]
     copies = [
-        pltpu.make_async_copy(src, dst, sems.at[i])
-        for i, (src, dst) in enumerate(
-            ((w_kv_at, w_kv), (tokens_at, tokens), (gain_at, gain), (w_query_at, w_query))
-        )
+        pltpu.make_async_copy(src, dst, sems.at[i]) for i, (src, dst) in enumerate(pairs)
     ]
     for copy in copies:
         copy.start()
@@ -71,14 +72,13 @@
         )
         for i in range(2)
     ]
-    copies[3].wait()
-    q = jnp.dot(normed, w_query[...], preferred_element_type=F32)
     stat = jnp.broadcast_to(jnp.sum(flat * flat, -1, keepdims=True), (rows, LANES))
     for half in range(2):
+        copies[3 + half].wait()
+        q = jnp.dot(normed, w_query[:, sides[half]], preferred_element_type=F32)
         for slot in range(8):
             if slot < 4:
-                at = (half * 4 + slot) * LANES
-                part = q[:, at : at + LANES]
+                part = q[:, slot * LANES : (slot + 1) * LANES]
             elif slot == 4:
                 part = kv[half]
             else:
@@ -207,7 +207,6 @@
                     line = jnp.floor(
                         pair[which][:, slot * LANES : (slot + 1) * LANES] * factor + 0.5
                     )
-                    line = jnp.clip(line, -TOP, TOP)
                 else:
                     line = jnp.broadcast_to(extras[which][slot - lines], (rows, LANES))
                 wide[pl.ds(half * 32 + which * 16 + slot, rows, stride=64), :] = line
@@ -257,7 +256,7 @@
         (tokens, norm_attn, w_query, w_kv),
         [ANY] * 4,
         [pltpu.VMEM(x.shape, x.dtype) for x in (tokens, norm_attn, w_query, w_kv)]
-        + [pltpu.VMEM((2 * width, hd), F32), pltpu.SemaphoreType.DMA((4,))],
+        + [pltpu.VMEM((2 * width, hd), F32), pltpu.SemaphoreType.DMA((5,))],
         60,
     )
     got = exchange(chunk.reshape(kv_count, 8, hd), "kv", FIRST)
@@ -302,7 +301,7 @@
         (hidden, w_down),
         scratch=[pltpu.VMEM((kv_count * 16, hd), F32)],
     )
-    got = exchange(part, "head", HEAD)
+    got = exchange(part, "head", LAST)
     layer_out = call(close, shape((steps, rollouts, width), BF16), (resid, got))
     return (layer_out, stored)
 

time: 113 us -> 113 us (level)
  no operation moved by 1% of the time
where the time goes in v8:
time: 113 us; the launch traced here: 112 us
  blocking collectives  87.5 us (77%)
  starting transfers between devices  13.3 us (12%)
  Pallas kernels  6.26 us (6%)
  local copies, waits for them, and re-layouts  4.39 us (4%)
    all_to_all x7, blocking collectives, exchange(): return lax.all_to_all(x, axis, 0, 0, tiled=True, axis_index_groups=[order])  87.5 us
    all_to_all x1, starting transfers between devices, exchange(): return lax.all_to_all(x, axis, 0, 0, tiled=True, axis_index_groups=[order])  13.3 us
    pallas_call x9, Pallas kernels, call(): pl.pallas_call(body, out_shape=out_shape, in_specs=[VMEM] * len(args) if...  6.26 us
    unnamed x19, local copies, waits for them, and re-layouts  4.39 us
  transfers between devices with their start and end apart: 1, of which 1 were waited for; matrix products, arithmetic and copies ran while one was open for 4% of the time, Pallas kernels for 0%

profile of v8, /device:TPU:1, one launch (start us, length us, event | category | flops | bytes accessed | tf_op | source)
XLA Modules:
  0.0 112.4 jit_solution(11681955958154803888)
XLA Ops:
  0.6 2.2 %shard_map.131 = f32[256,128]{1,0:T(8,128)} custom-call(bf16[2,8,256]{2,1,0:T(8,128)(2,1)} %tokens.1, bf16[256]{0:T(256)(128)(2,1)} %gain_at.1, bf16[256,1024]{1,0:T(8,128)(2,1)} %w_query_at.1, bf16[256,2,128]{2,1,0:T(2,128)(2,1)} %w_kv_at.1), custom_call_target="tpu_custom_call" | custom-call | tf_op jit(solution)/shard_map/pallas_call | solution.py:40
  2.8 13.3 %all-to-all-start = ((f32[32,8,128]{2,1,0:T(8,128)}), f32[32,8,128]{2,1,0:T(8,128)S(1)}, u32[]{:S(2)}, u32[]{:S(2)}) async-start(f32[32,8,128]{2,1,0:T(8,128)} %bitcast.11), calls=%async_computation | async-start | bytes 262144 | tf_op jit(solution)/shard_map/all_to_all | solution.py:36
  16.2 0.0 copy-start.1
  16.2 4.3 %copy.16 = bf16[256,2,3584]{2,0,1:T(8,128)(2,1)} copy(bf16[256,2,3584]{2,1,0:T(2,128)(2,1)} %param.18) | data formatting | bytes 7340032 | tf_op args[6]
  20.5 0.2 all-to-all-done.got
  20.7 0.0 copy-done.1
  20.8 11.4 %all_to_all.40.whole = bf16[32,8,128]{2,1,0:T(8,128)(2,1)S(1)} all-to-all(bf16[32,8,128]{2,1,0:T(8,128)(2,1)S(1)} %shard_map.132), channel_id=1, replica_groups={{144,152,128,136,176,184,160,168,208,216,192,200,240,248,224,232,16,24,..., dimensions={0} | all-to-all | bytes 131072 | tf_op jit(solution)/shard_map/all_to_all | solution.py:36
  32.2 0.0 copy-done.2
  32.2 0.0 copy-done.6
  32.2 0.0 copy-done.7
  32.2 0.0 copy-start.4
  32.2 0.0 copy-start
  32.2 0.0 copy-start.5
  32.2 0.0 copy-start.8
  32.2 1.5 %shard_map.133 = (f32[32,8,128]{2,1,0:T(8,128)S(1)}, bf16[1,2,8,1,2,128]{5,4,3,2,1,0:T(2,128)(2,1)}) custom-call(s32[8]{0:T(128)S(1)} %copy-done.6, s32[2]{0:T(128)S(1)} %copy-done.7, bf16[32,8,128]{2,1,0:T(8,128)(2,1)S(1)} %all_to_all.40.whole, bf16[8,1024,128]{2,1,0:T(8,128)(2,1)S(1)} %bitcast.10, bf16[8,1024,128]{2,1,0:T(8,128)(2,1)S(1)} %bitcast.9), custom_call_target="tpu_custom_call" | custom-call | tf_op jit(solution)/shard_map/pallas_call | solution.py:40
  33.7 12.3 %all_to_all.41.got = f32[32,8,128]{2,1,0:T(8,128)S(1)} all-to-all(f32[32,8,128]{2,1,0:T(8,128)S(1)} %get-tuple-element.6), channel_id=1, replica_groups={{144,152,128,136,176,184,160,168,208,216,192,200,240,248,224,232,16,24,..., dimensions={0} | all-to-all | bytes 262144 | tf_op jit(solution)/shard_map/all_to_all | solution.py:36
  46.0 0.2 shard_map.134
  46.2 11.7 %all_to_all.42.whole = bf16[32,4,128]{2,1,0:T(4,128)(2,1)S(1)} all-to-all(bf16[32,4,128]{2,1,0:T(4,128)(2,1)S(1)} %shard_map.134), channel_id=1, replica_groups={{144,152,128,136,176,184,160,168,208,216,192,200,240,248,224,232,16,24,..., dimensions={0} | all-to-all | bytes 65536 | tf_op jit(solution)/shard_map/all_to_all | solution.py:36
  57.9 0.0 copy-done.4
  57.9 0.2 shard_map.135
  58.1 12.9 %all_to_all.43.got = f32[8,16,256]{2,1,0:T(8,128)S(1)} all-to-all(f32[8,16,256]{2,1,0:T(8,128)S(1)} %shard_map.135), channel_id=1, replica_groups={{4,5,6,7,0,1,2,3},{12,13,14,15,8,9,10,11},{20,21,22,23,16,17,18,19},{28..., dimensions={0} | all-to-all | bytes 262144 | tf_op jit(solution)/shard_map/all_to_all | solution.py:36
  71.0 0.0 copy-done
  71.0 0.0 copy-done.5
  71.0 0.0 copy-done.8
  71.0 0.0 copy-start.3
  71.0 1.0 shard_map.136
  72.0 16.1 %all_to_all.44.got = s16[32,32,128]{2,1,0:T(8,128)(2,1)S(1)} all-to-all(s16[32,32,128]{2,1,0:T(8,128)(2,1)S(1)} %get-tuple-element.8), channel_id=1, replica_groups={{144,152,128,136,176,184,160,168,208,216,192,200,240,248,224,232,16,24,..., dimensions={0} | all-to-all | bytes 524288 | tf_op jit(solution)/shard_map/all_to_all | solution.py:36
  88.2 0.1 shard_map.137
  88.3 12.5 %all_to_all.45.whole = bf16[32,16,128]{2,1,0:T(8,128)(2,1)S(1)} all-to-all(bf16[32,16,128]{2,1,0:T(8,128)(2,1)S(1)} %shard_map.137), channel_id=1, replica_groups={{144,152,128,136,176,184,160,168,208,216,192,200,240,248,224,232,16,24,..., dimensions={0} | all-to-all | bytes 262144 | tf_op jit(solution)/shard_map/all_to_all | solution.py:36
  100.8 0.4 shard_map.138
  101.2 10.6 %all_to_all.46.got = f32[8,16,256]{2,1,0:T(8,128)S(1)} all-to-all(f32[8,16,256]{2,1,0:T(8,128)S(1)} %shard_map.138), channel_id=1, replica_groups={{4,5,2,6,3,7,0,1},{12,13,10,14,11,15,8,9},{20,21,18,22,19,23,16,17},{28..., dimensions={0} | all-to-all | bytes 262144 | tf_op jit(solution)/shard_map/all_to_all | solution.py:36
  111.8 0.6 shard_map.139
  (5 shorter events, 0.1 us)
Async XLA Ops:
  2.8 17.9 %all-to-all-start = ((f32[32,8,128]{2,1,0:T(8,128)}), f32[32,8,128]{2,1,0:T(8,128)S(1)}, u32[]{:S(2)}, u32[]{:S(2)}) async-start(f32[32,8,128]{2,1,0:T(8,128)} %bitcast.11), calls=%async_computation | async-start | bytes 262144 | tf_op jit(solution)/shard_map/all_to_all | solution.py:36
  16.2 4.6 %copy-start.1 = (bf16[8,1,1024,128]{3,2,1,0:T(8,128)(2,1)S(1)}, bf16[8,1,1024,128]{3,2,1,0:T(8,128)(2,1)}, u32[]{:S(2)}) copy-start(bf16[8,1,1024,128]{3,2,1,0:T(8,128)(2,1)} %param.21) | copy-start | bytes 6291460
  20.7 11.5 %copy-start.2 = (bf16[8,1,1024,128]{3,2,1,0:T(8,128)(2,1)S(1)}, bf16[8,1,1024,128]{3,2,1,0:T(8,128)(2,1)}, u32[]{:S(2)}) copy-start(bf16[8,1,1024,128]{3,2,1,0:T(8,128)(2,1)} %param.20) | copy-start | bytes 6291460
  20.7 11.5 %copy-start.6 = (s32[8]{0:T(128)S(1)}, s32[8]{0:T(128)}, u32[]{:S(2)}) copy-start(s32[8]{0:T(128)} %lengths.1) | copy-start | bytes 100
  20.7 11.5 %copy-start.7 = (s32[2]{0:T(128)S(1)}, s32[2]{0:T(128)}, u32[]{:S(2)}) copy-start(s32[2]{0:T(128)} %owner.1) | copy-start | bytes 28
  32.2 25.7 %copy-start.4 = (bf16[1024,256]{1,0:T(8,128)(2,1)S(1)}, bf16[1024,256]{1,0:T(8,128)(2,1)}, u32[]{:S(2)}) copy-start(bf16[1024,256]{1,0:T(8,128)(2,1)} %w.2) | copy-start | bytes 1572868
  32.2 38.8 %copy-start = (bf16[256,2,3584]{2,0,1:T(8,128)(2,1)S(1)}, bf16[256,2,3584]{2,0,1:T(8,128)(2,1)}, u32[]{:S(2)}) copy-start(bf16[256,2,3584]{2,0,1:T(8,128)(2,1)} %copy.16) | copy-start | bytes 11010052
  32.2 38.8 %copy-start.5 = (bf16[2,8,256]{2,1,0:T(8,128)(2,1)S(1)}, bf16[2,8,256]{2,1,0:T(8,128)(2,1)}, u32[]{:S(2)}) copy-start(bf16[2,8,256]{2,1,0:T(8,128)(2,1)} %tokens.1) | copy-start | bytes 24580
  32.2 38.7 %copy-start.8 = (bf16[256]{0:T(256)(128)(2,1)S(1)}, bf16[256]{0:T(256)(128)(2,1)}, u32[]{:S(2)}) copy-start(bf16[256]{0:T(256)(128)(2,1)} %gain.1) | copy-start | bytes 1540
  71.0 29.8 %copy-start.3 = (bf16[3584,256]{1,0:T(8,128)(2,1)S(1)}, bf16[3584,256]{1,0:T(8,128)(2,1)}, u32[]{:S(2)}) copy-start(bf16[3584,256]{1,0:T(8,128)(2,1)} %w.3) | copy-start | bytes 5505028

commit v9 on v3

--- a/solution.py
+++ b/solution.py
@@ -22,12 +22,12 @@
     major, minor = sizes
     return [
         (a + first[0]) % major * minor + (b + first[1]) % minor
+        for b in range(minor)
         for a in range(major)
-        for b in range(minor)
     ]
 
 
-ORDER = {"kv": ring((8, 4), (4, 2)), "head": ring((4, 2), (2, 0))}
+ORDER = {"kv": ring((8, 4), (4, 2)), "head": [4, 5, 6, 7, 0, 1, 2, 3]}
 
 
 def exchange(x, axis):

time: 113 us -> 113 us (level)
  no operation moved by 1% of the time
where the time goes in v9:
time: 113 us; the launch traced here: 112 us
  blocking collectives  87.2 us (77%)
  starting transfers between devices  13.9 us (12%)
  Pallas kernels  6.13 us (5%)
  local copies, waits for them, and re-layouts  4.39 us (4%)
    all_to_all x7, blocking collectives, exchange(): lax.all_to_all(x, axis, 0, 0, tiled=True, axis_index_groups=[ORDER[axis]])  87.2 us
    all_to_all x1, starting transfers between devices, exchange(): lax.all_to_all(x, axis, 0, 0, tiled=True, axis_index_groups=[ORDER[axis]])  13.9 us
    pallas_call x9, Pallas kernels, call(): pl.pallas_call(body, out_shape=out_shape, in_specs=[VMEM] * len(args) if...  6.13 us
    unnamed x19, local copies, waits for them, and re-layouts  4.39 us
  transfers between devices with their start and end apart: 1, of which 0 were waited for; matrix products, arithmetic and copies ran while one was open for 4% of the time, Pallas kernels for 0%

profile of v9, /device:TPU:1, one launch (start us, length us, event | category | flops | bytes accessed | tf_op | source)
XLA Modules:
  0.0 112.5 jit_solution(11767200548475814650)
XLA Ops:
  0.6 2.0 %shard_map.131 = f32[256,128]{1,0:T(8,128)} custom-call(bf16[2,8,256]{2,1,0:T(8,128)(2,1)} %tokens.1, bf16[256]{0:T(256)(128)(2,1)} %gain_at.1, bf16[256,1024]{1,0:T(8,128)(2,1)} %w_query_at.1, bf16[256,2,128]{2,1,0:T(2,128)(2,1)} %w_kv_at.1), custom_call_target="tpu_custom_call" | custom-call | tf_op jit(solution)/shard_map/pallas_call | solution.py:38
  2.7 13.9 %all-to-all-start = ((f32[32,8,128]{2,1,0:T(8,128)}), f32[32,8,128]{2,1,0:T(8,128)S(1)}, u32[]{:S(2)}, u32[]{:S(2)}) async-start(f32[32,8,128]{2,1,0:T(8,128)} %bitcast.11), calls=%async_computation | async-start | bytes 262144 | tf_op jit(solution)/shard_map/all_to_all | solution.py:34
  16.6 0.0 copy-start.1
  16.6 4.3 %copy.16 = bf16[256,2,3584]{2,0,1:T(8,128)(2,1)} copy(bf16[256,2,3584]{2,1,0:T(2,128)(2,1)} %param.18) | data formatting | bytes 7340032 | tf_op args[6]
  21.0 0.0 all-to-all-done.got
  21.0 0.0 copy-done.1
  21.0 0.0 copy-start.6
  21.0 0.0 copy-start.7
  21.0 11.4 %all_to_all.40.whole = bf16[32,8,128]{2,1,0:T(8,128)(2,1)S(1)} all-to-all(bf16[32,8,128]{2,1,0:T(8,128)(2,1)S(1)} %shard_map.132), channel_id=1, replica_groups={{144,176,208,240,16,48,80,112,152,184,216,248,24,56,88,120,128,160,192,..., dimensions={0} | all-to-all | bytes 131072 | tf_op jit(solution)/shard_map/all_to_all | solution.py:34
  32.5 0.0 copy-done.2
  32.5 0.0 copy-done.6
  32.5 0.0 copy-done.7
  32.5 0.0 copy-start.4
  32.5 0.0 copy-start
  32.5 0.0 copy-start.5
  32.5 0.0 copy-start.8
  32.5 1.5 %shard_map.133 = (f32[32,8,128]{2,1,0:T(8,128)S(1)}, bf16[1,2,8,1,2,128]{5,4,3,2,1,0:T(2,128)(2,1)}) custom-call(s32[8]{0:T(128)S(1)} %copy-done.6, s32[2]{0:T(128)S(1)} %copy-done.7, bf16[32,8,128]{2,1,0:T(8,128)(2,1)S(1)} %all_to_all.40.whole, bf16[8,1024,128]{2,1,0:T(8,128)(2,1)S(1)} %bitcast.10, bf16[8,1024,128]{2,1,0:T(8,128)(2,1)S(1)} %bitcast.9), custom_call_target="tpu_custom_call" | custom-call | tf_op jit(solution)/shard_map/pallas_call | solution.py:38
  34.0 12.5 %all_to_all.41.got = f32[32,8,128]{2,1,0:T(8,128)S(1)} all-to-all(f32[32,8,128]{2,1,0:T(8,128)S(1)} %get-tuple-element.6), channel_id=1, replica_groups={{144,176,208,240,16,48,80,112,152,184,216,248,24,56,88,120,128,160,192,..., dimensions={0} | all-to-all | bytes 262144 | tf_op jit(solution)/shard_map/all_to_all | solution.py:34
  46.6 0.2 shard_map.134
  46.7 11.4 %all_to_all.42.whole = bf16[32,4,128]{2,1,0:T(4,128)(2,1)S(1)} all-to-all(bf16[32,4,128]{2,1,0:T(4,128)(2,1)S(1)} %shard_map.134), channel_id=1, replica_groups={{144,176,208,240,16,48,80,112,152,184,216,248,24,56,88,120,128,160,192,..., dimensions={0} | all-to-all | bytes 65536 | tf_op jit(solution)/shard_map/all_to_all | solution.py:34
  58.2 0.0 copy-done.4
  58.2 0.2 shard_map.135
  58.4 12.7 %all_to_all.43.got = f32[8,16,256]{2,1,0:T(8,128)S(1)} all-to-all(f32[8,16,256]{2,1,0:T(8,128)S(1)} %shard_map.135), channel_id=1, replica_groups={{4,5,6,7,0,1,2,3},{12,13,14,15,8,9,10,11},{20,21,22,23,16,17,18,19},{28..., dimensions={0} | all-to-all | bytes 262144 | tf_op jit(solution)/shard_map/all_to_all | solution.py:34
  71.1 0.0 copy-done.5
  71.1 0.0 copy-start.3
  71.1 1.0 shard_map.136
  72.2 16.3 %all_to_all.44.got = s16[32,32,128]{2,1,0:T(8,128)(2,1)S(1)} all-to-all(s16[32,32,128]{2,1,0:T(8,128)(2,1)S(1)} %get-tuple-element.8), channel_id=1, replica_groups={{144,176,208,240,16,48,80,112,152,184,216,248,24,56,88,120,128,160,192,..., dimensions={0} | all-to-all | bytes 524288 | tf_op jit(solution)/shard_map/all_to_all | solution.py:34
  88.5 0.1 shard_map.137
  88.7 12.2 %all_to_all.45.whole = bf16[32,16,128]{2,1,0:T(8,128)(2,1)S(1)} all-to-all(bf16[32,16,128]{2,1,0:T(8,128)(2,1)S(1)} %shard_map.137), channel_id=1, replica_groups={{144,176,208,240,16,48,80,112,152,184,216,248,24,56,88,120,128,160,192,..., dimensions={0} | all-to-all | bytes 262144 | tf_op jit(solution)/shard_map/all_to_all | solution.py:34
  100.9 0.4 shard_map.138
  101.3 10.5 %all_to_all.46.got = f32[8,16,256]{2,1,0:T(8,128)S(1)} all-to-all(f32[8,16,256]{2,1,0:T(8,128)S(1)} %shard_map.138), channel_id=1, replica_groups={{4,5,6,7,0,1,2,3},{12,13,14,15,8,9,10,11},{20,21,22,23,16,17,18,19},{28..., dimensions={0} | all-to-all | bytes 262144 | tf_op jit(solution)/shard_map/all_to_all | solution.py:34
  111.8 0.6 shard_map.139
  (5 shorter events, 0.1 us)
Async XLA Ops:
  2.7 18.3 %all-to-all-start = ((f32[32,8,128]{2,1,0:T(8,128)}), f32[32,8,128]{2,1,0:T(8,128)S(1)}, u32[]{:S(2)}, u32[]{:S(2)}) async-start(f32[32,8,128]{2,1,0:T(8,128)} %bitcast.11), calls=%async_computation | async-start | bytes 262144 | tf_op jit(solution)/shard_map/all_to_all | solution.py:34
  16.6 4.4 %copy-start.1 = (bf16[8,1,1024,128]{3,2,1,0:T(8,128)(2,1)S(1)}, bf16[8,1,1024,128]{3,2,1,0:T(8,128)(2,1)}, u32[]{:S(2)}) copy-start(bf16[8,1,1024,128]{3,2,1,0:T(8,128)(2,1)} %param.21) | copy-start | bytes 6291460
  21.0 11.5 %copy-start.2 = (bf16[8,1,1024,128]{3,2,1,0:T(8,128)(2,1)S(1)}, bf16[8,1,1024,128]{3,2,1,0:T(8,128)(2,1)}, u32[]{:S(2)}) copy-start(bf16[8,1,1024,128]{3,2,1,0:T(8,128)(2,1)} %param.20) | copy-start | bytes 6291460
  21.0 11.5 %copy-start.6 = (s32[8]{0:T(128)S(1)}, s32[8]{0:T(128)}, u32[]{:S(2)}) copy-start(s32[8]{0:T(128)} %lengths.1) | copy-start | bytes 100
  21.0 11.5 %copy-start.7 = (s32[2]{0:T(128)S(1)}, s32[2]{0:T(128)}, u32[]{:S(2)}) copy-start(s32[2]{0:T(128)} %owner.1) | copy-start | bytes 28
  32.5 25.7 %copy-start.4 = (bf16[1024,256]{1,0:T(8,128)(2,1)S(1)}, bf16[1024,256]{1,0:T(8,128)(2,1)}, u32[]{:S(2)}) copy-start(bf16[1024,256]{1,0:T(8,128)(2,1)} %w.2) | copy-start | bytes 1572868
  32.5 38.6 %copy-start = (bf16[256,2,3584]{2,0,1:T(8,128)(2,1)S(1)}, bf16[256,2,3584]{2,0,1:T(8,128)(2,1)}, u32[]{:S(2)}) copy-start(bf16[256,2,3584]{2,0,1:T(8,128)(2,1)} %copy.16) | copy-start | bytes 11010052
  32.5 38.6 %copy-start.5 = (bf16[2,8,256]{2,1,0:T(8,128)(2,1)S(1)}, bf16[2,8,256]{2,1,0:T(8,128)(2,1)}, u32[]{:S(2)}) copy-start(bf16[2,8,256]{2,1,0:T(8,128)(2,1)} %tokens.1) | copy-start | bytes 24580
  32.5 38.6 %copy-start.8 = (bf16[256]{0:T(256)(128)(2,1)S(1)}, bf16[256]{0:T(256)(128)(2,1)}, u32[]{:S(2)}) copy-start(bf16[256]{0:T(256)(128)(2,1)} %gain.1) | copy-start | bytes 1540
  71.1 29.8 %copy-start.3 = (bf16[3584,256]{1,0:T(8,128)(2,1)S(1)}, bf16[3584,256]{1,0:T(8,128)(2,1)}, u32[]{:S(2)}) copy-start(bf16[3584,256]{1,0:T(8,128)(2,1)} %w.3) | copy-start | bytes 5505028

commit v10 on v6

--- a/solution.py
+++ b/solution.py
@@ -28,7 +28,7 @@
 
 
 FIRST, KV = ring((8, 4), (5, 2)), ring((8, 4), (4, 2))
-HEAD = [4, 5, 2, 6, 3, 7, 0, 1]
+HEAD = ring((4, 2), (2, 0))
 PLACE = [KV.index(device) for device in FIRST]
 
 

time: 113 us -> 112 us (level)
  no operation moved by 1% of the time
where the time goes in v10:
time: 112 us
  blocking collectives  87.2 us (78%)
  starting transfers between devices  13.3 us (12%)
  Pallas kernels  6.13 us (5%)
  local copies, waits for them, and re-layouts  4.39 us (4%)
    all_to_all x7, blocking collectives, exchange(): return lax.all_to_all(x, axis, 0, 0, tiled=True, axis_index_groups=[order])  87.2 us
    all_to_all x1, starting transfers between devices, exchange(): return lax.all_to_all(x, axis, 0, 0, tiled=True, axis_index_groups=[order])  13.3 us
    pallas_call x9, Pallas kernels, call(): pl.pallas_call(body, out_shape=out_shape, in_specs=[VMEM] * len(args) if...  6.13 us
    unnamed x19, local copies, waits for them, and re-layouts  4.39 us
  transfers between devices with their start and end apart: 1, of which 1 were waited for; matrix products, arithmetic and copies ran while one was open for 4% of the time, Pallas kernels for 0%

profile of v10, /device:TPU:1, one launch (start us, length us, event | category | flops | bytes accessed | tf_op | source)
XLA Modules:
  0.0 112.0 jit_solution(16628769570636960459)
XLA Ops:
  0.6 2.0 %shard_map.131 = f32[256,128]{1,0:T(8,128)} custom-call(bf16[2,8,256]{2,1,0:T(8,128)(2,1)} %tokens.1, bf16[256]{0:T(256)(128)(2,1)} %gain_at.1, bf16[256,1024]{1,0:T(8,128)(2,1)} %w_query_at.1, bf16[256,2,128]{2,1,0:T(2,128)(2,1)} %w_kv_at.1), custom_call_target="tpu_custom_call" | custom-call | tf_op jit(solution)/shard_map/pallas_call | solution.py:40
  2.7 13.3 %all-to-all-start = ((f32[32,8,128]{2,1,0:T(8,128)}), f32[32,8,128]{2,1,0:T(8,128)S(1)}, u32[]{:S(2)}, u32[]{:S(2)}) async-start(f32[32,8,128]{2,1,0:T(8,128)} %bitcast.11), calls=%async_computation | async-start | bytes 262144 | tf_op jit(solution)/shard_map/all_to_all | solution.py:36
  16.0 0.0 copy-start.1
  16.0 4.3 %copy.16 = bf16[256,2,3584]{2,0,1:T(8,128)(2,1)} copy(bf16[256,2,3584]{2,1,0:T(2,128)(2,1)} %param.18) | data formatting | bytes 7340032 | tf_op args[6]
  20.4 0.2 all-to-all-done.got
  20.6 0.0 copy-done.1
  20.6 11.4 %all_to_all.40.whole = bf16[32,8,128]{2,1,0:T(8,128)(2,1)S(1)} all-to-all(bf16[32,8,128]{2,1,0:T(8,128)(2,1)S(1)} %shard_map.132), channel_id=1, replica_groups={{144,152,128,136,176,184,160,168,208,216,192,200,240,248,224,232,16,24,..., dimensions={0} | all-to-all | bytes 131072 | tf_op jit(solution)/shard_map/all_to_all | solution.py:36
  32.0 0.0 copy-done.2
  32.1 0.0 copy-done.6
  32.1 0.0 copy-done.7
  32.1 0.0 copy-start.4
  32.1 0.0 copy-start
  32.1 0.0 copy-start.5
  32.1 0.0 copy-start.8
  32.1 1.5 %shard_map.133 = (f32[32,8,128]{2,1,0:T(8,128)S(1)}, bf16[1,2,8,1,2,128]{5,4,3,2,1,0:T(2,128)(2,1)}) custom-call(s32[8]{0:T(128)S(1)} %copy-done.6, s32[2]{0:T(128)S(1)} %copy-done.7, bf16[32,8,128]{2,1,0:T(8,128)(2,1)S(1)} %all_to_all.40.whole, bf16[8,1024,128]{2,1,0:T(8,128)(2,1)S(1)} %bitcast.10, bf16[8,1024,128]{2,1,0:T(8,128)(2,1)S(1)} %bitcast.9), custom_call_target="tpu_custom_call" | custom-call | tf_op jit(solution)/shard_map/pallas_call | solution.py:40
  33.6 12.3 %all_to_all.41.got = f32[32,8,128]{2,1,0:T(8,128)S(1)} all-to-all(f32[32,8,128]{2,1,0:T(8,128)S(1)} %get-tuple-element.6), channel_id=1, replica_groups={{144,152,128,136,176,184,160,168,208,216,192,200,240,248,224,232,16,24,..., dimensions={0} | all-to-all | bytes 262144 | tf_op jit(solution)/shard_map/all_to_all | solution.py:36
  45.9 0.2 shard_map.134
  46.1 11.7 %all_to_all.42.whole = bf16[32,4,128]{2,1,0:T(4,128)(2,1)S(1)} all-to-all(bf16[32,4,128]{2,1,0:T(4,128)(2,1)S(1)} %shard_map.134), channel_id=1, replica_groups={{144,152,128,136,176,184,160,168,208,216,192,200,240,248,224,232,16,24,..., dimensions={0} | all-to-all | bytes 65536 | tf_op jit(solution)/shard_map/all_to_all | solution.py:36
  57.7 0.0 copy-done.4
  57.7 0.2 shard_map.135
  57.9 12.9 %all_to_all.43.got = f32[8,16,256]{2,1,0:T(8,128)S(1)} all-to-all(f32[8,16,256]{2,1,0:T(8,128)S(1)} %shard_map.135), channel_id=1, replica_groups={{4,5,6,7,0,1,2,3},{12,13,14,15,8,9,10,11},{20,21,22,23,16,17,18,19},{28..., dimensions={0} | all-to-all | bytes 262144 | tf_op jit(solution)/shard_map/all_to_all | solution.py:36
  70.8 0.0 copy-done
  70.8 0.0 copy-done.8
  70.8 0.0 copy-start.3
  70.9 1.0 shard_map.136
  71.9 16.1 %all_to_all.44.got = s16[32,32,128]{2,1,0:T(8,128)(2,1)S(1)} all-to-all(s16[32,32,128]{2,1,0:T(8,128)(2,1)S(1)} %get-tuple-element.8), channel_id=1, replica_groups={{144,152,128,136,176,184,160,168,208,216,192,200,240,248,224,232,16,24,..., dimensions={0} | all-to-all | bytes 524288 | tf_op jit(solution)/shard_map/all_to_all | solution.py:36
  88.0 0.1 shard_map.137
  88.2 12.5 %all_to_all.45.whole = bf16[32,16,128]{2,1,0:T(8,128)(2,1)S(1)} all-to-all(bf16[32,16,128]{2,1,0:T(8,128)(2,1)S(1)} %shard_map.137), channel_id=1, replica_groups={{144,152,128,136,176,184,160,168,208,216,192,200,240,248,224,232,16,24,..., dimensions={0} | all-to-all | bytes 262144 | tf_op jit(solution)/shard_map/all_to_all | solution.py:36
  100.7 0.0 copy-done.3
  100.7 0.4 shard_map.138
  101.1 10.4 %all_to_all.46.got = f32[8,16,256]{2,1,0:T(8,128)S(1)} all-to-all(f32[8,16,256]{2,1,0:T(8,128)S(1)} %shard_map.138), channel_id=1, replica_groups={{4,5,6,7,0,1,2,3},{12,13,14,15,8,9,10,11},{20,21,22,23,16,17,18,19},{28..., dimensions={0} | all-to-all | bytes 262144 | tf_op jit(solution)/shard_map/all_to_all | solution.py:36
  111.4 0.6 shard_map.139
  (5 shorter events, 0.1 us)
Async XLA Ops:
  2.7 17.9 %all-to-all-start = ((f32[32,8,128]{2,1,0:T(8,128)}), f32[32,8,128]{2,1,0:T(8,128)S(1)}, u32[]{:S(2)}, u32[]{:S(2)}) async-start(f32[32,8,128]{2,1,0:T(8,128)} %bitcast.11), calls=%async_computation | async-start | bytes 262144 | tf_op jit(solution)/shard_map/all_to_all | solution.py:36
  16.0 4.6 %copy-start.1 = (bf16[8,1,1024,128]{3,2,1,0:T(8,128)(2,1)S(1)}, bf16[8,1,1024,128]{3,2,1,0:T(8,128)(2,1)}, u32[]{:S(2)}) copy-start(bf16[8,1,1024,128]{3,2,1,0:T(8,128)(2,1)} %param.21) | copy-start | bytes 6291460
  20.6 11.5 %copy-start.2 = (bf16[8,1,1024,128]{3,2,1,0:T(8,128)(2,1)S(1)}, bf16[8,1,1024,128]{3,2,1,0:T(8,128)(2,1)}, u32[]{:S(2)}) copy-start(bf16[8,1,1024,128]{3,2,1,0:T(8,128)(2,1)} %param.20) | copy-start | bytes 6291460
  20.6 11.5 %copy-start.6 = (s32[8]{0:T(128)S(1)}, s32[8]{0:T(128)}, u32[]{:S(2)}) copy-start(s32[8]{0:T(128)} %lengths.1) | copy-start | bytes 100
  20.6 11.5 %copy-start.7 = (s32[2]{0:T(128)S(1)}, s32[2]{0:T(128)}, u32[]{:S(2)}) copy-start(s32[2]{0:T(128)} %owner.1) | copy-start | bytes 28
  32.1 25.7 %copy-start.4 = (bf16[1024,256]{1,0:T(8,128)(2,1)S(1)}, bf16[1024,256]{1,0:T(8,128)(2,1)}, u32[]{:S(2)}) copy-start(bf16[1024,256]{1,0:T(8,128)(2,1)} %w.2) | copy-start | bytes 1572868
  32.1 38.8 %copy-start = (bf16[256,2,3584]{2,0,1:T(8,128)(2,1)S(1)}, bf16[256,2,3584]{2,0,1:T(8,128)(2,1)}, u32[]{:S(2)}) copy-start(bf16[256,2,3584]{2,0,1:T(8,128)(2,1)} %copy.16) | copy-start | bytes 11010052
  32.1 38.8 %copy-start.5 = (bf16[2,8,256]{2,1,0:T(8,128)(2,1)S(1)}, bf16[2,8,256]{2,1,0:T(8,128)(2,1)}, u32[]{:S(2)}) copy-start(bf16[2,8,256]{2,1,0:T(8,128)(2,1)} %tokens.1) | copy-start | bytes 24580
  32.1 38.7 %copy-start.8 = (bf16[256]{0:T(256)(128)(2,1)S(1)}, bf16[256]{0:T(256)(128)(2,1)}, u32[]{:S(2)}) copy-start(bf16[256]{0:T(256)(128)(2,1)} %gain.1) | copy-start | bytes 1540
  70.8 29.8 %copy-start.3 = (bf16[3584,256]{1,0:T(8,128)(2,1)S(1)}, bf16[3584,256]{1,0:T(8,128)(2,1)}, u32[]{:S(2)}) copy-start(bf16[3584,256]{1,0:T(8,128)(2,1)} %w.3) | copy-start | bytes 5505028
